TPU v7x, 32 devices: a whole 2x2x4 slice. The times are simulated.
32 devices in a mesh: ctx: 16 (over z, y, x), tp: 2 (over core).
Axes of the slice: x: 2, y: 2, z: 4, core: 2. Of those that a mesh axis runs over, the one named last changes fastest.
Arguments:
- signal: float32 [4096, 2048], P('tp', 'ctx'), may hold values from -0.03125 to 0.03125
- cotangent: float32 [4096, 2048], P('tp', 'ctx'), may hold values from -6 to 6
- filters: float32 [256, 2048], P(None, 'ctx'), may hold values from -0.125 to 0.125
Outputs:
- grad_signal: float32 [4096, 2048], P('tp', 'ctx')
- grad_filters: float32 [256, 2048], P(None, 'ctx')
All inputs are finite; a program needn't handle non-finite values.
Results may differ from a plain program's by a relative error of at most 0.0001.
Values sent between devices are 32-bit elements; how exact they have to be, the bound alone decides.
No kernel may reach another device: no remote copies, remote signals or barrier semaphores. Data moves between devices by JAX's collectives and lax.ppermute only.
A program may use at most 128 MiB of HBM per device.

v0:
```python
import math

import jax
import jax.numpy as jnp
from jax import lax
from jax.sharding import PartitionSpec as P

precise = lax.Precision.HIGHEST


def angle_table(rows_idx, cols_idx, modulus):
    product = rows_idx[:, None] * cols_idx[None, :] % modulus
    return product.astype(jnp.float32) * (2.0 * math.pi / modulus)


def forward_inner(blocks, cos_in, sin_in, twid_cos, twid_sin):
    real_part = jnp.einsum("csi,ks->cki", blocks, cos_in, precision=precise)
    imag_part = -jnp.einsum("csi,ks->cki", blocks, sin_in, precision=precise)
    return jnp.stack(
        [real_part * twid_cos + imag_part * twid_sin, imag_part * twid_cos - real_part * twid_sin]
    )


def inverse_outer(spectra, cos_out, sin_out, back_cos, back_sin):
    real_in, imag_in = (spectra[0], spectra[1])
    real_part = jnp.einsum("cjk,kn->cjn", real_in, cos_out, precision=precise) - jnp.einsum(
        "cjk,kn->cjn", imag_in, sin_out, precision=precise
    )
    imag_part = jnp.einsum("cjk,kn->cjn", imag_in, cos_out, precision=precise) + jnp.einsum(
        "cjk,kn->cjn", real_in, sin_out, precision=precise
    )
    return jnp.stack(
        [real_part * back_cos - imag_part * back_sin, imag_part * back_cos + real_part * back_sin]
    )


def inverse_inner(spectra, cos_in, sin_in):
    return jnp.einsum("ckn,kp->cpn", spectra[0], cos_in, precision=precise) - jnp.einsum(
        "ckn,kp->cpn", spectra[1], sin_in, precision=precise
    )


def body(signal, cotangent, filters):
    ctx_count = lax.axis_size("ctx")
    ctx_rank = lax.axis_index("ctx")
    local_len = signal.shape[1]
    total_len = 2 * ctx_count * local_len
    chan_local = signal.shape[0]
    filt_count = filters.shape[0]
    src_idx = jnp.arange(ctx_count, dtype=jnp.int32)
    freq_idx = jnp.arange(2 * ctx_count, dtype=jnp.int32)
    inner_angle = angle_table(freq_idx, src_idx, 2 * ctx_count)
    cos_in = jnp.cos(inner_angle)
    sin_in = jnp.sin(inner_angle)
    pos_idx = jnp.arange(local_len, dtype=jnp.int32)
    outer_angle = angle_table(pos_idx, pos_idx, local_len)
    cos_out = jnp.cos(outer_angle)
    sin_out = jnp.sin(outer_angle)
    scale_back = 1.0 / total_len
    chan_idx = lax.axis_index("tp") * chan_local + jnp.arange(chan_local, dtype=jnp.int32)
    selector = (
        chan_idx[:, None] % filt_count == jnp.arange(filt_count, dtype=jnp.int32)[None, :]
    ).astype(jnp.float32)
    piece_len = local_len // ctx_count
    own_pos = ctx_rank * piece_len + jnp.arange(piece_len, dtype=jnp.int32)
    twid_angle = angle_table(freq_idx, own_pos, total_len)
    twid_cos = jnp.cos(twid_angle)
    twid_sin = jnp.sin(twid_angle)
    own_freq = 2 * ctx_rank + jnp.arange(2, dtype=jnp.int32)
    back_angle = angle_table(own_freq, pos_idx, total_len)
    back_cos = jnp.cos(back_angle)
    back_sin = jnp.sin(back_angle)
    sig_blocks, cot_blocks, fil_blocks = (
        lax.all_to_all(
            signal.reshape(chan_local, 1, local_len), "ctx", split_axis=2, concat_axis=1, tiled=True
        ),
        lax.all_to_all(
            cotangent.reshape(chan_local, 1, local_len),
            "ctx",
            split_axis=2,
            concat_axis=1,
            tiled=True,
        ),
        lax.all_to_all(
            filters.reshape(filt_count, 1, local_len),
            "ctx",
            split_axis=2,
            concat_axis=1,
            tiled=True,
        ),
    )
    sig_part = forward_inner(sig_blocks, cos_in, sin_in, twid_cos, twid_sin)
    cot_part = forward_inner(cot_blocks, cos_in, sin_in, twid_cos, twid_sin)
    fil_part = forward_inner(fil_blocks, cos_in, sin_in, twid_cos, twid_sin)
    sig_part, cot_part, fil_part = (
        lax.all_to_all(sig_part, "ctx", split_axis=2, concat_axis=3, tiled=True),
        lax.all_to_all(cot_part, "ctx", split_axis=2, concat_axis=3, tiled=True),
        lax.all_to_all(fil_part, "ctx", split_axis=2, concat_axis=3, tiled=True),
    )
    joined = jnp.concatenate([sig_part, cot_part, fil_part], axis=1)
    real_in, imag_in = (joined[0], joined[1])
    spec_real = jnp.einsum("cjn,nk->cjk", real_in, cos_out, precision=precise) + jnp.einsum(
        "cjn,nk->cjk", imag_in, sin_out, precision=precise
    )
    spec_imag = jnp.einsum("cjn,nk->cjk", imag_in, cos_out, precision=precise) - jnp.einsum(
        "cjn,nk->cjk", real_in, sin_out, precision=precise
    )
    sig_real, cot_real, fil_real = (
        spec_real[:chan_local],
        spec_real[chan_local : 2 * chan_local],
        spec_real[2 * chan_local :],
    )
    sig_imag, cot_imag, fil_imag = (
        spec_imag[:chan_local],
        spec_imag[chan_local : 2 * chan_local],
        spec_imag[2 * chan_local :],
    )
    chan_fil_real = jnp.einsum("cf,fjk->cjk", selector, fil_real, precision=precise)
    chan_fil_imag = jnp.einsum("cf,fjk->cjk", selector, fil_imag, precision=precise)
    dsig_spec = jnp.stack(
        [
            chan_fil_real * cot_real + chan_fil_imag * cot_imag,
            chan_fil_real * cot_imag - chan_fil_imag * cot_real,
        ]
    )
    prod_real = sig_real * cot_real + sig_imag * cot_imag
    prod_imag = sig_real * cot_imag - sig_imag * cot_real
    dfil_spec = jnp.stack(
        [
            jnp.einsum("cf,cjk->fjk", selector, prod_real, precision=precise),
            jnp.einsum("cf,cjk->fjk", selector, prod_imag, precision=precise),
        ]
    )
    filt_rows = dfil_spec.shape[1]
    combined = jnp.concatenate([dsig_spec, dfil_spec], axis=1)
    finished = inverse_outer(combined, cos_out, sin_out, back_cos, back_sin)
    dsig_part, dfil_part = (
        lax.all_to_all(finished[:, :chan_local], "ctx", split_axis=3, concat_axis=2, tiled=True),
        lax.all_to_all(finished[:, chan_local:], "ctx", split_axis=3, concat_axis=2, tiled=True),
    )
    dsig_pos = inverse_inner(dsig_part, cos_in, sin_in)
    dfil_pos = inverse_inner(dfil_part, cos_in, sin_in)
    dsig_pos, dfil_pos = (
        lax.all_to_all(dsig_pos, "ctx", split_axis=1, concat_axis=2, tiled=True),
        lax.all_to_all(dfil_pos, "ctx", split_axis=1, concat_axis=2, tiled=True),
    )
    grad_signal = dsig_pos.reshape(chan_local, local_len) * scale_back
    grad_part = dfil_pos.reshape(filt_rows, local_len) * scale_back
    grad_filters = lax.psum(grad_part, "tp")
    return (grad_signal, grad_filters)


def solution(mesh):
    return jax.shard_map(
        body,
        mesh=mesh,
        in_specs=(P("tp", "ctx"), P("tp", "ctx"), P(None, "ctx")),
        out_specs=(P("tp", "ctx"), P(None, "ctx")),
        check_vma=False,
    )
```

profile of v0, /device:TPU:0, one launch (start us, length us, event | category | flops | bytes accessed | tf_op | source)
XLA Modules:
  0.0 528.5 jit_solution(530064762683162618)
XLA Ops:
  7.2 1.7 copy.112
  8.9 8.3 %all-to-all-start.4 = ((f32[256,1,128]{0,1,2:T(1,128)}), f32[256,1,128]{0,1,2:T(1,128)S(1)}, u32[]{:S(2)}, u32[]{:S(2)}) async-start(f32[256,1,128]{0,1,2:T(1,128)} %copy.112), calls=%async_computation.4 | async-start | bytes 262144 | tf_op jit(solution)/shard_map/all_to_all | solution.py:84
  17.2 3.7 copy.110
  20.9 4.1 all-to-all-done.4
  25.0 3.7 all-to-all-start.2
  28.7 1.9 copy.108
  30.6 21.4 %all-to-all-done.2 = f32[2048,1,128]{0,1,2:T(1,128)S(1)} async-done(((f32[2048,1,128]{0,1,2:T(1,128)}), f32[2048,1,128]{0,1,2:T(1,128)S(1)}, u32[]{:S(2)}, u32[]{:S(2)}) %all-to-all-start.2) | async-done | bytes 1048608 | tf_op jit(solution)/shard_map/all_to_all | solution.py:77
  52.0 5.8 %all-to-all-start = ((f32[2048,1,128]{0,1,2:T(1,128)}), f32[2048,1,128]{0,1,2:T(1,128)S(1)}, u32[]{:S(2)}, u32[]{:S(2)}) async-start(f32[2048,1,128]{0,1,2:T(1,128)} %copy.108), calls=%async_computation | async-start | bytes 2097152 | tf_op jit(solution)/shard_map/all_to_all | solution.py:74
  59.0 1.1 copy.85
  60.4 2.2 convolution_negate_fusion
  62.7 3.6 fusion.45
  66.2 14.4 %all-to-all-done = f32[2048,1,128]{0,1,2:T(1,128)S(1)} async-done(((f32[2048,1,128]{0,1,2:T(1,128)}), f32[2048,1,128]{0,1,2:T(1,128)S(1)}, u32[]{:S(2)}, u32[]{:S(2)}) %all-to-all-start) | async-done | bytes 1048608 | tf_op jit(solution)/shard_map/all_to_all | solution.py:74
  80.6 6.3 %all-to-all-start.5 = ((f32[2,256,32,8]{1,3,0,2:T(8,128)}), f32[2,256,32,8]{1,3,0,2:T(8,128)}, u32[]{:S(2)}, u32[]{:S(2)}) async-start(f32[2,256,32,8]{1,3,0,2:T(8,128)} %copy.85), calls=%async_computation.5 | async-start | bytes 1048576 | tf_op jit(solution)/shard_map/all_to_all | solution.py:98
  87.3 2.2 convolution_negate_fusion.1
  89.5 4.4 add_bitcast_fusion.3
  94.5 4.5 copy.73
  98.9 1.7 all-to-all-done.5
  100.6 5.5 %all-to-all-start.1 = ((f32[2,2048,32,8]{1,3,0,2:T(8,128)}), f32[2,2048,32,8]{1,3,0,2:T(8,128)}, u32[]{:S(2)}, u32[]{:S(2)}) async-start(f32[2,2048,32,8]{1,3,0,2:T(8,128)} %copy.73), calls=%async_computation.1 | async-start | bytes 8388608 | tf_op jit(solution)/shard_map/all_to_all | solution.py:96
  106.1 2.0 pad_maximum_fusion.2
  108.1 4.4 copy.79
  112.5 71.3 %all-to-all-done.1 = f32[2,2048,32,8]{1,3,0,2:T(8,128)} async-done(((f32[2,2048,32,8]{1,3,0,2:T(8,128)}), f32[2,2048,32,8]{1,3,0,2:T(8,128)}, u32[]{:S(2)}, u32[]{:S(2)}) %all-to-all-start.1) | async-done | bytes 4194336 | tf_op jit(solution)/shard_map/all_to_all | solution.py:96
  183.8 18.2 %all-to-all-start.3 = ((f32[2,2048,32,8]{1,3,0,2:T(8,128)}), f32[2,2048,32,8]{1,3,0,2:T(8,128)}, u32[]{:S(2)}, u32[]{:S(2)}) async-start(f32[2,2048,32,8]{1,3,0,2:T(8,128)} %copy.79), calls=%async_computation.3 | async-start | bytes 8388608 | tf_op jit(solution)/shard_map/all_to_all | solution.py:97
  202.2 1.1 copy.147
  203.5 4.6 copy.143
  208.1 5.4 %copy.88 = f32[2,2048,2,128]{3,1,2,0:T(8,128)} copy(f32[2,2048,2,128]{1,3,2,0:T(8,128)} %bitcast.175) | data formatting | bytes 8388608 | tf_op jit(solution)/shard_map/all_to_all | solution.py:96
  213.5 67.0 %all-to-all-done.3 = f32[2,2048,32,8]{1,3,0,2:T(8,128)} async-done(((f32[2,2048,32,8]{1,3,0,2:T(8,128)}), f32[2,2048,32,8]{1,3,0,2:T(8,128)}, u32[]{:S(2)}, u32[]{:S(2)}) %all-to-all-start.3) | async-done | bytes 4194336 | tf_op jit(solution)/shard_map/all_to_all | solution.py:97
  280.5 4.7 copy.142
  285.2 5.4 %copy.89 = f32[2,2048,2,128]{3,1,2,0:T(8,128)} copy(f32[2,2048,2,128]{1,3,2,0:T(8,128)} %bitcast.176) | data formatting | bytes 8388608 | tf_op jit(solution)/shard_map/all_to_all | solution.py:97
  290.6 4.2 pad_maximum_fusion
  294.8 4.1 fusion.1
  298.9 4.1 fusion.2
  303.0 4.2 convolution_add_fusion
  307.2 4.1 convolution_subtract_fusion
  311.3 1.8 fusion.17
  313.2 1.6 fusion.29
  314.8 1.6 fusion.34
  316.4 2.2 add_bitcast_fusion.1
  319.0 2.6 fusion.5
  321.6 2.3 fusion.4
  323.9 2.4 convolution_add_fusion.1
  326.4 2.7 add_bitcast_fusion
  329.1 1.4 copy-done
  330.5 1.0 copy.98
  331.5 19.2 %all-to-all-start.8 = ((f32[2,256,2,128]{1,2,0,3:T(2,128)}), f32[2,256,2,128]{1,2,0,3:T(2,128)S(1)}, u32[]{:S(2)}, u32[]{:S(2)}) async-start(f32[2,256,2,128]{1,2,0,3:T(2,128)} %copy.98), calls=%async_computation.8 | async-start | bytes 1048576 | tf_op jit(solution)/shard_map/all_to_all | solution.py:139
  350.7 3.8 fusion
  354.5 7.3 %copy.93 = f32[2,2048,2,128]{1,2,0,3:T(2,128)} copy(f32[2,2048,2,128]{3,1,2,0:T(8,128)} %fusion) | data formatting | bytes 8388608 | tf_op jit(solution)/shard_map/slice | solution.py:138
  361.8 3.2 all-to-all-done.8
  365.1 4.5 all-to-all-start.6
  371.2 0.7 copy.102
  372.0 76.0 %all-to-all-done.6 = f32[2,2048,2,128]{1,2,0,3:T(2,128)} async-done(((f32[2,2048,2,128]{1,2,0,3:T(2,128)}), f32[2,2048,2,128]{1,2,0,3:T(2,128)}, u32[]{:S(2)}, u32[]{:S(2)}) %all-to-all-start.6) | async-done | bytes 4194336 | tf_op jit(solution)/shard_map/all_to_all | solution.py:138
  448.0 18.5 %all-to-all-start.9 = ((f32[256,16,8]{0,2,1:T(8,128)}), f32[256,16,8]{0,2,1:T(8,128)S(1)}, u32[]{:S(2)}, u32[]{:S(2)}) async-start(f32[256,16,8]{0,2,1:T(8,128)} %copy.102), calls=%async_computation.9 | async-start | bytes 262144 | tf_op jit(solution)/shard_map/all_to_all | solution.py:145
  466.5 4.6 copy.144
  471.1 1.7 fusion.198
  472.8 1.6 copy.95
  474.5 2.4 squeeze.28
  476.9 2.9 fusion.90
  479.8 3.0 copy.96
  482.8 2.7 squeeze.29
  485.5 1.1 fusion.3
  486.6 1.6 copy.97
  488.2 7.0 %all-to-all-start.7 = ((f32[2048,16,8]{0,2,1:T(8,128)}), f32[2048,16,8]{0,2,1:T(8,128)S(1)}, u32[]{:S(2)}, u32[]{:S(2)}) async-start(f32[2048,16,8]{0,2,1:T(8,128)} %copy.97), calls=%async_computation.7 | async-start | bytes 2097152 | tf_op jit(solution)/shard_map/all_to_all | solution.py:144
  496.0 22.2 %all-reduce.2.cloned.1.call-done = f32[256,128]{0,1:T(8,128)} async-done(((f32[256,128]{0,1:T(8,128)}), f32[256,128]{0,1:T(8,128)}) %all-reduce.2.cloned.1.call-update) | async-done | bytes 131088 | tf_op jit(solution)/shard_map/psum | solution.py:149
  518.2 1.7 copy.104
  519.9 1.3 copy.103
  (38 shorter events, 5.4 us)
Async XLA Ops:
  7.2 21.5 %copy-start.4 = (f32[2048,128]{1,0:T(8,128)S(1)}, f32[2048,128]{1,0:T(8,128)}, u32[]{:S(2)}) copy-start(f32[2048,128]{1,0:T(8,128)} %param.3) | copy-start | bytes 3145732
  8.9 16.1 %all-to-all-start.4 = ((f32[256,1,128]{0,1,2:T(1,128)}), f32[256,1,128]{0,1,2:T(1,128)S(1)}, u32[]{:S(2)}, u32[]{:S(2)}) async-start(f32[256,1,128]{0,1,2:T(1,128)} %copy.112), calls=%async_computation.4 | async-start | bytes 262144 | tf_op jit(solution)/shard_map/all_to_all | solution.py:84
  25.0 26.9 %all-to-all-start.2 = ((f32[2048,1,128]{0,1,2:T(1,128)}), f32[2048,1,128]{0,1,2:T(1,128)S(1)}, u32[]{:S(2)}, u32[]{:S(2)}) async-start(f32[2048,1,128]{0,1,2:T(1,128)} %copy.110), calls=%async_computation.2 | async-start | bytes 2097152 | tf_op jit(solution)/shard_map/all_to_all | solution.py:77
  52.0 28.7 %all-to-all-start = ((f32[2048,1,128]{0,1,2:T(1,128)}), f32[2048,1,128]{0,1,2:T(1,128)S(1)}, u32[]{:S(2)}, u32[]{:S(2)}) async-start(f32[2048,1,128]{0,1,2:T(1,128)} %copy.108), calls=%async_computation | async-start | bytes 2097152 | tf_op jit(solution)/shard_map/all_to_all | solution.py:74
  80.6 20.0 %all-to-all-start.5 = ((f32[2,256,32,8]{1,3,0,2:T(8,128)}), f32[2,256,32,8]{1,3,0,2:T(8,128)}, u32[]{:S(2)}, u32[]{:S(2)}) async-start(f32[2,256,32,8]{1,3,0,2:T(8,128)} %copy.85), calls=%async_computation.5 | async-start | bytes 1048576 | tf_op jit(solution)/shard_map/all_to_all | solution.py:98
  86.9 2.6 copy-start.1
  98.9 7.2 %copy-start.2 = (f32[1,2048,32,8]{1,2,3,0:T(8,128)S(1)}, f32[1,2048,32,8]{1,2,3,0:T(8,128)}, u32[]{:S(2)}) copy-start(f32[1,2048,32,8]{1,2,3,0:T(8,128)} %get-tuple-element.22) | copy-start | bytes 6291460
  100.6 83.2 %all-to-all-start.1 = ((f32[2,2048,32,8]{1,3,0,2:T(8,128)}), f32[2,2048,32,8]{1,3,0,2:T(8,128)}, u32[]{:S(2)}, u32[]{:S(2)}) async-start(f32[2,2048,32,8]{1,3,0,2:T(8,128)} %copy.73), calls=%async_computation.1 | async-start | bytes 8388608 | tf_op jit(solution)/shard_map/all_to_all | solution.py:96
  183.8 96.7 %all-to-all-start.3 = ((f32[2,2048,32,8]{1,3,0,2:T(8,128)}), f32[2,2048,32,8]{1,3,0,2:T(8,128)}, u32[]{:S(2)}, u32[]{:S(2)}) async-start(f32[2,2048,32,8]{1,3,0,2:T(8,128)} %copy.79), calls=%async_computation.3 | async-start | bytes 8388608 | tf_op jit(solution)/shard_map/all_to_all | solution.py:97
  329.1 1.4 copy-start
  331.5 33.6 %all-to-all-start.8 = ((f32[2,256,2,128]{1,2,0,3:T(2,128)}), f32[2,256,2,128]{1,2,0,3:T(2,128)S(1)}, u32[]{:S(2)}, u32[]{:S(2)}) async-start(f32[2,256,2,128]{1,2,0,3:T(2,128)} %copy.98), calls=%async_computation.8 | async-start | bytes 1048576 | tf_op jit(solution)/shard_map/all_to_all | solution.py:139
  365.1 82.9 %all-to-all-start.6 = ((f32[2,2048,2,128]{1,2,0,3:T(2,128)}), f32[2,2048,2,128]{1,2,0,3:T(2,128)}, u32[]{:S(2)}, u32[]{:S(2)}) async-start(f32[2,2048,2,128]{1,2,0,3:T(2,128)} %copy.93), calls=%async_computation.6 | async-start | bytes 8388608 | tf_op jit(solution)/shard_map/all_to_all | solution.py:138
  448.0 40.2 %all-to-all-start.9 = ((f32[256,16,8]{0,2,1:T(8,128)}), f32[256,16,8]{0,2,1:T(8,128)S(1)}, u32[]{:S(2)}, u32[]{:S(2)}) async-start(f32[256,16,8]{0,2,1:T(8,128)} %copy.102), calls=%async_computation.9 | async-start | bytes 262144 | tf_op jit(solution)/shard_map/all_to_all | solution.py:145
  476.9 2.9 copy-start.3
  488.2 31.6 %all-to-all-start.7 = ((f32[2048,16,8]{0,2,1:T(8,128)}), f32[2048,16,8]{0,2,1:T(8,128)S(1)}, u32[]{:S(2)}, u32[]{:S(2)}) async-start(f32[2048,16,8]{0,2,1:T(8,128)} %copy.97), calls=%async_computation.7 | async-start | bytes 2097152 | tf_op jit(solution)/shard_map/all_to_all | solution.py:144
  495.2 23.0 %all-reduce.2.cloned.1.call-start = ((), (), s32[]{:S(2)}) async-start(), calls=%async_computation.10 | async-start | bytes 262144 | tf_op jit(solution)/shard_map/psum | solution.py:149
Sparse Core Ops, SparseCore 0:
  498.9 19.1 all-reduce.1
where the time goes:
time: 536 us; the launch traced here: 529 us
  waiting for transfers between devices  281 us (52%)
  starting transfers between devices  97 us (18%)
  local copies, waits for them, and re-layouts  71.3 us (13%)
  matrix products  51.9 us (10%)
  between operations  15 us (3%)
  other arithmetic  11.9 us (2%)
    all_to_all x1, waiting for transfers between devices, body(): lax.all_to_all(finished[:, :chan_local], 'ctx', split_axis=3, concat_axis...  76 us
    all_to_all x1, waiting for transfers between devices, body(): lax.all_to_all(sig_part, 'ctx', split_axis=2, concat_axis=3, tiled=True)  71.3 us
    all_to_all x1, waiting for transfers between devices, body(): lax.all_to_all(cot_part, 'ctx', split_axis=2, concat_axis=3, tiled=True)  67 us
    psum x1, waiting for transfers between devices, body(): grad_filters = lax.psum(grad_part, 'tp')  22.2 us
    all_to_all x1, waiting for transfers between devices, body(): lax.all_to_all(cotangent.reshape(chan_local, 1, local_len), 'ctx', split_...  21.4 us
    all_to_all x1, starting transfers between devices, body(): lax.all_to_all(finished[:, chan_local:], 'ctx', split_axis=3, concat_axis...  19.2 us
    all_to_all x1, starting transfers between devices, body(): lax.all_to_all(dfil_pos, 'ctx', split_axis=1, concat_axis=2, tiled=True)  18.5 us
    all_to_all x1, starting transfers between devices, body(): lax.all_to_all(cot_part, 'ctx', split_axis=2, concat_axis=3, tiled=True)  18.2 us
  transfers between devices with their start and end apart: 11, of which 9 were waited for; matrix products, arithmetic and copies ran while one was open for 15% of the time, Pallas kernels for 0%

commit v1 on v0

v1 whole, which is shorter than its diff:
```python
import functools

import jax
import jax.numpy as jnp
from jax import lax
from jax.experimental import pallas as pl
from jax.experimental.pallas import tpu as pltpu
from jax.sharding import PartitionSpec as P

f32, bf16 = jnp.float32, jnp.bfloat16
PAIR = 256


def split_two(value):
    high = value.astype(bf16)
    low = (value - high.astype(f32)).astype(bf16)
    return high, low


def load_rows(ref, filt, blocks, group, filts):
    pieces = [ref[b, pl.ds(filt, group, stride=filts), :] for b in range(blocks)]
    even = jnp.concatenate(pieces[0::2], axis=0)
    odd = jnp.concatenate(pieces[1::2], axis=0)
    return jnp.concatenate([even, odd], axis=1)


def left_fill_roll(value, shift):
    lanes = lax.broadcasted_iota(jnp.int32, value.shape, 1)
    return jnp.where(lanes >= shift, pltpu.roll(value, shift, 1), 0.0)


def signal_kernel(blocks, group, filts, cot_ref, fil_ref, out_ref, high_ref, low_ref):
    local = cot_ref.shape[2]
    pairs = blocks // 2
    length = blocks * local

    def one_filter(filt, carry):
        rows = load_rows(cot_ref, filt, blocks, group, filts)
        lags = jnp.concatenate([fil_ref[b, pl.ds(filt, 1), :] for b in range(blocks)], axis=1)
        first = pltpu.roll(jnp.broadcast_to(lags, (8, length)), 0, 1, stride=1, stride_axis=0)
        lane = lax.broadcasted_iota(jnp.int32, (8, length), 1)
        row = lax.broadcasted_iota(jnp.int32, (8, length), 0)
        first = jnp.where(lane >= row, first, 0.0)
        for step in range(local // 16):
            two = jnp.concatenate(
                [left_fill_roll(first, 16 * step), left_fill_roll(first, 16 * step + 8)], axis=0
            )
            high, low = split_two(two)
            high_ref[pl.ds(16 * step, 16), :] = high
            low_ref[pl.ds(16 * step, 16), :] = low
            pad = jnp.zeros((16, local), bf16)
            high_ref[pl.ds(local + 16 * step, 16), :] = jnp.concatenate([pad, high[:, : length - local]], axis=1)
            low_ref[pl.ds(local + 16 * step, 16), :] = jnp.concatenate([pad, low[:, : length - local]], axis=1)
        total = None
        nt = (((1,), (1,)), ((), ()))
        for gap in range(pairs):
            high, low = split_two(rows[gap * group :, :])
            t_high = high_ref[:, pl.ds(gap * PAIR, PAIR)]
            t_low = low_ref[:, pl.ds(gap * PAIR, PAIR)]
            part = (
                lax.dot_general(high, t_high, nt, preferred_element_type=f32)
                + lax.dot_general(low, t_high, nt, preferred_element_type=f32)
                + lax.dot_general(high, t_low, nt, preferred_element_type=f32)
            )
            if total is None:
                total = part
            else:
                part = jnp.concatenate([part, jnp.zeros((gap * group, PAIR), f32)], axis=0)
                total = total + part
        for b in range(blocks):
            piece = total[(b // 2) * group : (b // 2 + 1) * group, (b % 2) * local : (b % 2 + 1) * local]
            out_ref[b, pl.ds(filt, group, stride=filts), :] = piece
        return carry

    lax.fori_loop(0, filts, one_filter, 0)


def filter_kernel(blocks, group, filts, cot_ref, sig_ref, out_ref, prod_ref):
    local = cot_ref.shape[2]
    pairs = blocks // 2

    def one_filter(filt, carry):
        cot = load_rows(cot_ref, filt, blocks, group, filts)
        sig = load_rows(sig_ref, filt, blocks, group, filts)
        sig_high = sig.astype(bf16).astype(f32)
        stacked = jnp.concatenate([sig_high, sig_high, sig - sig_high], axis=0)
        turned = stacked.T.astype(bf16)
        cot_high = cot.astype(bf16).astype(f32)
        cot_low = cot - cot_high
        for gap in range(pairs):
            pieces = []
            for part in (cot_high, cot_low, cot_high):
                pieces.append(part[gap * group :, :])
                if gap:
                    pieces.append(jnp.zeros((gap * group, PAIR), f32))
            weights = jnp.concatenate(pieces, axis=0).astype(bf16)
            prod_ref[gap] = jnp.dot(turned, weights, preferred_element_type=f32)
        lane = lax.broadcasted_iota(jnp.int32, (8, PAIR), 1)
        sub = lax.broadcasted_iota(jnp.int32, (8, PAIR), 0)
        for gap in range(pairs):
            total = jnp.zeros((8, PAIR), f32)
            for step in reversed(range(PAIR // 8)):
                here = prod_ref[gap, pl.ds(8 * step, 8), :]
                if gap + 1 < pairs:
                    after = prod_ref[gap + 1, pl.ds(8 * step, 8), :]
                else:
                    after = jnp.zeros((8, PAIR), f32)
                kept = jnp.where(lane >= sub + 8 * step, here, after)
                total = pltpu.roll(total, PAIR - 8, 1) + kept
            for bit in (1, 2, 4):
                total = jnp.where((sub & bit) != 0, pltpu.roll(total, PAIR - bit, 1), total)
            total = jnp.sum(total, axis=0, keepdims=True)
            out_ref[2 * gap, pl.ds(filt, 1), :] = total[:, :local]
            out_ref[2 * gap + 1, pl.ds(filt, 1), :] = total[:, local:]
        return carry

    lax.fori_loop(0, filts, one_filter, 0)


def call_signal(cot, fil, group):
    blocks, _, local = cot.shape
    filts = fil.shape[1]
    flops = 2 * 3 * filts * group * (blocks * local) ** 2 // 2
    return pl.pallas_call(
        functools.partial(signal_kernel, blocks, group, filts),
        out_shape=jax.ShapeDtypeStruct(cot.shape, f32),
        in_specs=[pl.BlockSpec(memory_space=pltpu.VMEM)] * 2,
        out_specs=pl.BlockSpec(memory_space=pltpu.VMEM),
        scratch_shapes=[pltpu.VMEM((PAIR, blocks * local), bf16)] * 2,
        compiler_params=pltpu.CompilerParams(vmem_limit_bytes=40 << 20),
        cost_estimate=pl.CostEstimate(flops=flops, bytes_accessed=8 * cot.size, transcendentals=0),
        name="grad_signal",
    )(cot, fil)


def call_filter(cot, sig, group):
    blocks, rows, local = cot.shape
    filts = rows // group
    flops = 2 * 3 * rows * (blocks * local) ** 2
    return pl.pallas_call(
        functools.partial(filter_kernel, blocks, group, filts),
        out_shape=jax.ShapeDtypeStruct((blocks, filts, local), f32),
        in_specs=[pl.BlockSpec(memory_space=pltpu.VMEM)] * 2,
        out_specs=pl.BlockSpec(memory_space=pltpu.VMEM),
        scratch_shapes=[pltpu.VMEM((blocks // 2, PAIR, PAIR), f32)],
        compiler_params=pltpu.CompilerParams(vmem_limit_bytes=40 << 20),
        cost_estimate=pl.CostEstimate(flops=flops, bytes_accessed=8 * cot.size, transcendentals=0),
        name="grad_filters",
    )(cot, sig)


def exchange(value):
    return lax.all_to_all(value, "ctx", split_axis=0, concat_axis=0, tiled=True)


def body(signal, cotangent, filters):
    ranks = lax.axis_size("ctx")
    channels, local = signal.shape
    count = filters.shape[0]
    group = channels // count
    filts = count // ranks

    def by_owner(value):
        return value.reshape(group, ranks, filts, local).transpose(1, 0, 2, 3).reshape(ranks, group * filts, local)

    first = exchange(jnp.concatenate([by_owner(cotangent), filters.reshape(ranks, filts, local)], axis=1))
    sig = exchange(by_owner(signal))
    cot, fil = first[:, : group * filts], first[:, group * filts :]
    dsig = exchange(call_signal(cot, fil, group))
    dfil = call_filter(cot, sig, group)
    if lax.axis_size("tp") == 2:
        dfil = dfil + lax.ppermute(dfil, "tp", [(0, 1), (1, 0)])
    else:
        dfil = lax.psum(dfil, "tp")
    dfil = exchange(dfil)
    grad_signal = dsig.reshape(ranks, group, filts, local).transpose(1, 0, 2, 3).reshape(channels, local)
    return grad_signal, dfil.reshape(count, local)


def solution(mesh):
    return jax.shard_map(
        body,
        mesh=mesh,
        in_specs=(P("tp", "ctx"), P("tp", "ctx"), P(None, "ctx")),
        out_specs=(P("tp", "ctx"), P(None, "ctx")),
        check_vma=False,
    )
```

time: 536 us -> 176 us (0.33); the launches traced: 529 us -> 175 us
  waiting for transfers between devices: 281 us -> 74.6 us
  starting transfers between devices: 97 us -> 27.4 us
  local copies, waits for them, and re-layouts: 71.3 us -> 4.28 us
  Pallas kernels: 0 us -> 66.5 us
  matrix products: 51.9 us -> 0 us
  between operations: 15 us -> 0.73 us
  other arithmetic: 11.9 us -> 1.77 us
    all_to_all x10 -> x4, waiting for transfers between devices: 259 us -> 73.2 us  [exchange(): return lax.all_to_all(value, 'ctx', split_axis=0, concat_axis=0, tiled=True)]
    all_to_all x10 -> x4, starting transfers between devices: 96.9 us -> 27.3 us  [exchange(): return lax.all_to_all(value, 'ctx', split_axis=0, concat_axis=0, tiled=True)]
    pallas_call x0 -> x2, Pallas kernels: none -> 66.5 us  [the longest x1 45.9 us: call_filter(): pl.pallas_call(functools.partial(filter_kernel, blocks, group, filts), ou...]
    dot_general x22 -> x0, matrix products: 51.9 us -> none  [the longest x3 8.54 us: forward_inner(): real_part = jnp.einsum('csi,ks->cki', blocks, cos_in, precision=precise)]
    all_to_all x8 -> x0, local copies, waits for them, and re-layouts: 26 us -> none  [the longest x2 10.1 us: body(): lax.all_to_all(cot_part, 'ctx', split_axis=2, concat_axis=3, tiled=True)]
    psum x1 -> x0, waiting for transfers between devices: 22.2 us -> none  [body(): grad_filters = lax.psum(grad_part, 'tp')]
    slice x8 -> x2, local copies, waits for them, and re-layouts: 15.1 us -> 0.11 us  [body(): cot, fil = (first[:, :group * filts], first[:, group * filts:])]
    another operation x3 -> x0, local copies, waits for them, and re-layouts: 10 us -> none  [forward_inner(): jnp.stack([real_part * twid_cos + imag_part * twid_sin, imag_part * twid_...]
  transfers between devices with their start and end apart: 11 -> 5, of which waited for: 9 -> 4; matrix products, arithmetic and copies ran while one was open for 15% -> 1% of each run, Pallas kernels for 0% -> 12%
where the time goes in v1:
time: 176 us; the launch traced here: 175 us
  waiting for transfers between devices  74.6 us (42%)
  Pallas kernels  66.5 us (38%)
  starting transfers between devices  27.4 us (16%)
  local copies, waits for them, and re-layouts  4.28 us (2%)
  other arithmetic  1.77 us (1%)
    all_to_all x4, waiting for transfers between devices, exchange(): return lax.all_to_all(value, 'ctx', split_axis=0, concat_axis=0, tiled=True)  73.2 us
    pallas_call x1, Pallas kernels, call_filter(): pl.pallas_call(functools.partial(filter_kernel, blocks, group, filts), ou...  45.9 us
    all_to_all x4, starting transfers between devices, exchange(): return lax.all_to_all(value, 'ctx', split_axis=0, concat_axis=0, tiled=True)  27.3 us
    pallas_call x1, Pallas kernels, call_signal(): pl.pallas_call(functools.partial(signal_kernel, blocks, group, filts), ou...  20.6 us
  transfers between devices with their start and end apart: 5, of which 4 were waited for; matrix products, arithmetic and copies ran while one was open for 1% of the time, Pallas kernels for 12%

profile of v1, /device:TPU:0, one launch (start us, length us, event | category | flops | bytes accessed | tf_op | source)
XLA Modules:
  0.0 175.3 jit_solution(18408138576416888271)
XLA Ops:
  0.6 0.0 copy-start.1
  0.6 1.4 copy.5
  2.0 0.0 copy-done.1
  2.0 1.1 pad_maximum_fusion
  3.1 0.0 copy-start
  3.1 8.4 %all-to-all-start = ((f32[16,144,128]{2,1,0:T(8,128)}), f32[16,144,128]{2,1,0:T(8,128)S(1)}, u32[]{:S(2)}, u32[]{:S(2)}) async-start(f32[16,144,128]{2,1,0:T(8,128)} %pad_maximum_fusion), calls=%async_computation | async-start | bytes 2359296 | tf_op jit(solution)/shard_map/all_to_all | solution.py:153
  11.6 0.0 copy-done
  11.6 1.1 copy.7
  12.7 25.9 %all-to-all-done = f32[16,144,128]{2,1,0:T(8,128)S(1)} async-done(((f32[16,144,128]{2,1,0:T(8,128)}), f32[16,144,128]{2,1,0:T(8,128)S(1)}, u32[]{:S(2)}, u32[]{:S(2)}) %all-to-all-start) | async-done | bytes 1179680 | tf_op jit(solution)/shard_map/all_to_all | solution.py:153
  38.6 6.1 %all-to-all-start.2 = ((f32[16,128,128]{2,1,0:T(8,128)}), f32[16,128,128]{2,1,0:T(8,128)S(1)}, u32[]{:S(2)}, u32[]{:S(2)}) async-start(f32[16,128,128]{2,1,0:T(8,128)} %bitcast.9), calls=%async_computation.2 | async-start | bytes 2097152 | tf_op jit(solution)/shard_map/all_to_all | solution.py:153
  44.7 0.1 slice.8.cot_ref
  44.8 23.1 %all-to-all-done.2.sig_ref = f32[16,128,128]{2,1,0:T(8,128)S(1)} async-done(((f32[16,128,128]{2,1,0:T(8,128)}), f32[16,128,128]{2,1,0:T(8,128)S(1)}, u32[]{:S(2)}, u32[]{:S(2)}) %all-to-all-start.2) | async-done | bytes 1048608 | tf_op jit(solution)/shard_map/all_to_all | solution.py:153
  67.9 45.9 %grad_filters.1 = f32[16,16,128]{2,1,0:T(8,128)S(1)} custom-call(f32[16,128,128]{2,1,0:T(8,128)S(1)} %slice.8.cot_ref, f32[16,128,128]{2,1,0:T(8,128)S(1)} %all-to-all-done.2.sig_ref), custom_call_target="tpu_custom_call" | custom-call | flops 3221225472 | bytes 2097152 | tf_op jit(solution)/shard_map/grad_filters/pallas_call | solution.py:140
  113.9 0.1 collective-permute-start
  113.9 1.3 collective-permute-done
  115.3 0.7 add.3
  115.9 5.9 %all-to-all-start.3 = ((f32[16,16,128]{2,1,0:T(8,128)}), f32[16,16,128]{2,1,0:T(8,128)S(1)}, u32[]{:S(2)}, u32[]{:S(2)}) async-start(f32[16,16,128]{2,1,0:T(8,128)} %add.3), calls=%async_computation.3 | async-start | bytes 262144 | tf_op jit(solution)/shard_map/all_to_all | solution.py:153
  121.9 20.6 %grad_signal.1 = f32[16,128,128]{2,1,0:T(8,128)} custom-call(f32[16,128,128]{2,1,0:T(8,128)S(1)} %slice.8.cot_ref, f32[16,16,128]{2,1,0:T(8,128)S(1)} %slice.9.fil_ref), custom_call_target="tpu_custom_call" | custom-call | flops 1610612736 | bytes 2097152 | tf_op jit(solution)/shard_map/grad_signal/pallas_call | solution.py:124
  142.4 0.0 all-to-all-done.3
  142.4 6.9 %all-to-all-start.1 = ((f32[16,128,128]{2,1,0:T(8,128)}), f32[16,128,128]{2,1,0:T(8,128)S(1)}, u32[]{:S(2)}, u32[]{:S(2)}) async-start(f32[16,128,128]{2,1,0:T(8,128)} %grad_signal.1), calls=%async_computation.1 | async-start | bytes 2097152 | tf_op jit(solution)/shard_map/all_to_all | solution.py:153
  149.4 24.2 %all-to-all-done.1 = f32[16,128,128]{2,1,0:T(8,128)S(1)} async-done(((f32[16,128,128]{2,1,0:T(8,128)}), f32[16,128,128]{2,1,0:T(8,128)S(1)}, u32[]{:S(2)}, u32[]{:S(2)}) %all-to-all-start.1) | async-done | bytes 1048608 | tf_op jit(solution)/shard_map/all_to_all | solution.py:153
  173.5 1.1 copy.6
  174.6 0.7 copy.9
  (1 shorter events, 0.0 us)
Async XLA Ops:
  0.6 1.4 copy-start.1
  3.1 8.5 %copy-start = (f32[2048,128]{1,0:T(8,128)S(1)}, f32[2048,128]{1,0:T(8,128)}, u32[]{:S(2)}) copy-start(f32[2048,128]{1,0:T(8,128)} %param.3) | copy-start | bytes 3145732
  3.1 35.5 %all-to-all-start = ((f32[16,144,128]{2,1,0:T(8,128)}), f32[16,144,128]{2,1,0:T(8,128)S(1)}, u32[]{:S(2)}, u32[]{:S(2)}) async-start(f32[16,144,128]{2,1,0:T(8,128)} %pad_maximum_fusion), calls=%async_computation | async-start | bytes 2359296 | tf_op jit(solution)/shard_map/all_to_all | solution.py:153
  38.6 29.3 %all-to-all-start.2 = ((f32[16,128,128]{2,1,0:T(8,128)}), f32[16,128,128]{2,1,0:T(8,128)S(1)}, u32[]{:S(2)}, u32[]{:S(2)}) async-start(f32[16,128,128]{2,1,0:T(8,128)} %bitcast.9), calls=%async_computation.2 | async-start | bytes 2097152 | tf_op jit(solution)/shard_map/all_to_all | solution.py:153
  113.9 1.4 collective-permute-start
  115.9 26.5 %all-to-all-start.3 = ((f32[16,16,128]{2,1,0:T(8,128)}), f32[16,16,128]{2,1,0:T(8,128)S(1)}, u32[]{:S(2)}, u32[]{:S(2)}) async-start(f32[16,16,128]{2,1,0:T(8,128)} %add.3), calls=%async_computation.3 | async-start | bytes 262144 | tf_op jit(solution)/shard_map/all_to_all | solution.py:153
  142.4 31.1 %all-to-all-start.1 = ((f32[16,128,128]{2,1,0:T(8,128)}), f32[16,128,128]{2,1,0:T(8,128)S(1)}, u32[]{:S(2)}, u32[]{:S(2)}) async-start(f32[16,128,128]{2,1,0:T(8,128)} %grad_signal.1), calls=%async_computation.1 | async-start | bytes 2097152 | tf_op jit(solution)/shard_map/all_to_all | solution.py:153

commit v2 on v1

v2 whole, which is shorter than its diff:
```python
import functools

import jax
import jax.numpy as jnp
from jax import lax
from jax.experimental import pallas as pl
from jax.experimental.pallas import tpu as pltpu
from jax.sharding import PartitionSpec as P

f32, bf16 = jnp.float32, jnp.bfloat16
PAIR = 256


def split_two(value):
    high = value.astype(bf16)
    low = (value - high.astype(f32)).astype(bf16)
    return high, low


def rotate_left(value, shift):
    half = value.shape[1] // 2
    if shift == half:
        return jnp.concatenate([value[:, half:], value[:, :half]], axis=1)
    return pltpu.roll(value, value.shape[1] - shift, 1)


def load_blocks(ref, start, blocks, sources, group):
    pieces = []
    for b in range(blocks):
        for s in range(sources):
            pieces.append(ref[b * sources + s, pl.ds(start, group), :])
    even = jnp.concatenate([p for at, p in enumerate(pieces) if at // sources % 2 == 0], axis=0)
    odd = jnp.concatenate([p for at, p in enumerate(pieces) if at // sources % 2 == 1], axis=0)
    return jnp.concatenate([even, odd], axis=1)


def gradients_kernel(plan, first_filt, last_filt, *refs):
    blocks, sources, group, filts, early = plan
    if first_filt == 0:
        fil_ref, data_ref, out_ref, strip_high, strip_low, cot_high, cot_low, prod_ref = refs
        fil_at = 2 * early * group
    else:
        fil_ref, data_ref, done_ref, out_ref, strip_high, strip_low, cot_high, cot_low, prod_ref = refs
        fil_at = 2 * early * group
        out_ref[...] = done_ref[...]
    local = data_ref.shape[2]
    count = last_filt - first_filt
    pairs = blocks // 2
    step_rows = sources * group
    rows_all = pairs * step_rows
    length = blocks * local
    held = cot_high.dtype
    flip = lax.broadcasted_iota(jnp.int32, (local, local), 0) + lax.broadcasted_iota(jnp.int32, (local, local), 1)
    flip = jnp.where(flip == local - 1, 1.0, 0.0).astype(bf16)
    for ref in (cot_high, cot_low):
        ref[pl.ds(rows_all, rows_all), :] = jnp.zeros((rows_all, PAIR), held)
    prod_ref[pairs] = jnp.zeros((PAIR, PAIR), f32)
    lane = lax.broadcasted_iota(jnp.int32, (8, PAIR), 1)
    sub = lax.broadcasted_iota(jnp.int32, (8, PAIR), 0)
    ahead = lane - sub

    def one_filter(turn, carry):
        filt = first_filt + turn
        rows = load_blocks(data_ref, turn * group, blocks, sources, group)
        high, low = split_two(rows)
        cot_high[pl.ds(0, rows_all), :] = high.astype(held)
        cot_low[pl.ds(0, rows_all), :] = low.astype(held)

        lags = [fil_ref[b * sources, pl.ds(fil_at + filt, 1), :] for b in reversed(range(blocks))]
        high, low = split_two(jnp.concatenate(lags, axis=0))
        back = jnp.dot(high, flip, preferred_element_type=f32) + jnp.dot(low, flip, preferred_element_type=f32)
        back = [jnp.broadcast_to(back[b : b + 1, :], (8, local)) for b in range(blocks)]
        back = jnp.concatenate(back + [jnp.zeros((8, PAIR), f32)], axis=1)
        skewed = pltpu.roll(back, 1, 1, stride=1, stride_axis=0)
        for step in range(local // 16):
            two = jnp.concatenate([pltpu.roll(skewed, 16 * step, 1), pltpu.roll(skewed, 16 * step + 8, 1)], axis=0)
            high, low = split_two(two)
            strip_high[pl.ds(16 * step, 16), :] = high
            strip_low[pl.ds(16 * step, 16), :] = low

        sig = load_blocks(data_ref, (count + turn) * group, blocks, sources, group).T
        sig_high, sig_low = split_two(sig)
        turned = jnp.concatenate([sig_high, sig_high, sig_low], axis=1)
        for gap in range(pairs):
            high = cot_high[pl.ds(gap * step_rows, rows_all), :].astype(bf16)
            low = cot_low[pl.ds(gap * step_rows, rows_all), :].astype(bf16)
            weights = jnp.concatenate([high, low, high], axis=0)
            prod_ref[gap] = jnp.dot(turned, weights, preferred_element_type=f32)

        total = None
        for gap in range(pairs):
            kept = rows_all - gap * step_rows
            high = cot_high[pl.ds(gap * step_rows, kept), :].astype(bf16)
            low = cot_low[pl.ds(gap * step_rows, kept), :].astype(bf16)
            at = length - gap * PAIR
            t_high = jnp.concatenate([strip_high[:, pl.ds(at, PAIR)], strip_high[:, pl.ds(at - local, PAIR)]], axis=0)
            t_low = jnp.concatenate([strip_low[:, pl.ds(at, PAIR)], strip_low[:, pl.ds(at - local, PAIR)]], axis=0)
            part = (
                jnp.dot(high, t_high, preferred_element_type=f32)
                + jnp.dot(low, t_high, preferred_element_type=f32)
                + jnp.dot(high, t_low, preferred_element_type=f32)
            )
            if total is None:
                total = part
            else:
                part = jnp.concatenate([part, jnp.zeros((gap * step_rows, PAIR), f32)], axis=0)
                total = total + part
        for b in range(blocks):
            for s in range(sources):
                at = b // 2 * step_rows + s * group
                piece = total[at : at + group, b % 2 * local : (b % 2 + 1) * local]
                out_ref[b * sources + s, pl.ds(filt * group, group), :] = piece

        def folded(gap, step, steps):
            if steps == 1:
                here = prod_ref[gap, pl.ds(8 * step, 8), :]
                after = prod_ref[gap + 1, pl.ds(8 * step, 8), :]
                return jnp.where(ahead >= 8 * step, here, after)
            half = steps // 2
            return folded(gap, step, half) + rotate_left(folded(gap, step + half, half), 8 * half)

        for gap in range(pairs):
            lagged = folded(gap, 0, PAIR // 8)
            for bit in (1, 2, 4):
                lagged = jnp.where((sub & bit) != 0, rotate_left(lagged, bit), lagged)
            lagged = jnp.sum(lagged, axis=0, keepdims=True)
            for s in range(sources):
                out_ref[2 * gap * sources + s, pl.ds(filts * group + filt, 1), :] = lagged[:, :local]
                out_ref[(2 * gap + 1) * sources + s, pl.ds(filts * group + filt, 1), :] = lagged[:, local:]
        return carry

    lax.fori_loop(0, count, one_filter, 0)


def vmem_call(kernel, outs, args, name, flops, scratch=()):
    return pl.pallas_call(
        kernel,
        out_shape=outs,
        in_specs=[pl.BlockSpec(memory_space=pltpu.VMEM)] * len(args),
        out_specs=jax.tree.map(lambda _: pl.BlockSpec(memory_space=pltpu.VMEM), outs),
        scratch_shapes=list(scratch),
        compiler_params=pltpu.CompilerParams(vmem_limit_bytes=44 << 20),
        cost_estimate=pl.CostEstimate(
            flops=int(flops), bytes_accessed=sum(4 * a.size for a in args), transcendentals=0
        ),
        name=name,
    )(*args)


def call_gradients(plan, first_filt, last_filt, *args):
    blocks, sources, group, filts, early = plan
    local = args[0].shape[2]
    rows = blocks * sources * group
    held = bf16 if sources * group % 16 == 0 else f32
    scratch = (
        [pltpu.VMEM((local, blocks * local + PAIR), bf16)] * 2
        + [pltpu.VMEM((rows, PAIR), held)] * 2
        + [pltpu.VMEM((blocks // 2 + 1, PAIR, PAIR), f32)]
    )
    outs = jax.ShapeDtypeStruct((blocks * sources, filts * group + filts, local), f32)
    kernel = functools.partial(gradients_kernel, plan, first_filt, last_filt)
    flops = (last_filt - first_filt) * 3e9
    return vmem_call(kernel, outs, args, "gradients", flops, scratch)


def pack_kernel(plan, owners, cot_ref, sig_ref, fil_ref, early_ref, late_ref):
    _, _, group, filts, early = plan
    count = owners * filts

    def one_owner(owner, carry):
        for filt in range(filts):
            ref, at, many = (early_ref, filt, early) if filt < early else (late_ref, filt - early, filts - early)
            for part, source in enumerate((cot_ref, sig_ref)):
                rows = source[pl.ds(owner * filts + filt, group, stride=count), :]
                ref[owner, pl.ds((part * many + at) * group, group), :] = rows
        early_ref[owner, pl.ds(2 * early * group, filts), :] = fil_ref[pl.ds(owner * filts, filts), :]
        return carry

    lax.fori_loop(0, owners, one_owner, 0)


def unpack_kernel(plan, owners, in_ref, sig_ref, fil_ref):
    _, _, group, filts, _ = plan
    count = owners * filts

    def one_owner(owner, carry):
        for filt in range(filts):
            sig_ref[pl.ds(owner * filts + filt, group, stride=count), :] = in_ref[owner, pl.ds(filt * group, group), :]
        fil_ref[pl.ds(owner * filts, filts), :] = in_ref[owner, pl.ds(filts * group, filts), :]
        return carry

    lax.fori_loop(0, owners, one_owner, 0)


def body(signal, cotangent, filters):
    ranks, halves = lax.axis_size("ctx"), lax.axis_size("tp")
    channels, local = signal.shape
    count = filters.shape[0]
    both = count % (8 * ranks * halves) == 0
    axes, sources = (("ctx", "tp"), halves) if both else ("ctx", 1)
    owners = ranks * sources
    group, filts = channels // count, count // owners
    early = filts - filts // 4
    plan = (ranks, sources, group, filts, early)

    def exchange(value):
        return lax.all_to_all(value, axes, split_axis=0, concat_axis=0, tiled=True)

    sizes = (2 * early * group + filts, 2 * (filts - early) * group)
    sends = vmem_call(
        functools.partial(pack_kernel, plan, owners),
        [jax.ShapeDtypeStruct((owners, rows, local), f32) for rows in sizes],
        (cotangent, signal, filters),
        "pack_rows",
        1e6,
    )
    first = exchange(sends[0])
    first, late = lax.optimization_barrier((first, sends[1]))
    second = exchange(late)
    grads = call_gradients(plan, 0, early, first, first)
    grads = call_gradients(plan, early, filts, first, second, grads)
    grad_signal, grad_filters = vmem_call(
        functools.partial(unpack_kernel, plan, owners),
        [jax.ShapeDtypeStruct((channels, local), f32), jax.ShapeDtypeStruct((count, local), f32)],
        (exchange(grads),),
        "unpack_rows",
        1e6,
    )
    if not both:
        grad_filters = lax.psum(grad_filters, "tp")
    return grad_signal, grad_filters


def solution(mesh):
    return jax.shard_map(
        body,
        mesh=mesh,
        in_specs=(P("tp", "ctx"), P("tp", "ctx"), P(None, "ctx")),
        out_specs=(P("tp", "ctx"), P(None, "ctx")),
        check_vma=False,
    )
```

time: 176 us -> 112 us (0.64)
  blocking collectives: 0 us -> 81 us
  waiting for transfers between devices: 74.6 us -> 4.42 us
  Pallas kernels: 66.5 us -> 18.8 us
  starting transfers between devices: 27.4 us -> 3.51 us
  other arithmetic: 1.77 us -> 0 us
    all_to_all x0 -> x2, blocking collectives: none -> 81 us  [exchange(): return lax.all_to_all(value, axes, split_axis=0, concat_axis=0, tiled=True)]
    all_to_all x4 -> x1, waiting for transfers between devices: 73.2 us -> 4.42 us  [exchange(): return lax.all_to_all(value, axes, split_axis=0, concat_axis=0, tiled=True)]
    pallas_call x2 -> x4, Pallas kernels: 66.5 us -> 18.8 us  [vmem_call(): pl.pallas_call(kernel, out_shape=outs, in_specs=[pl.BlockSpec(memory_spac...]
    all_to_all x4 -> x1, starting transfers between devices: 27.3 us -> 3.51 us  [exchange(): return lax.all_to_all(value, axes, split_axis=0, concat_axis=0, tiled=True)]
    unnamed x5 -> x6, local copies, waits for them, and re-layouts: 0.66 us -> 3.35 us
    reshape x2 -> x0, local copies, waits for them, and re-layouts: 2.44 us -> none  [by_owner(): value.reshape(group, ranks, filts, local).transpose(1, 0, 2, 3)]
  transfers between devices with their start and end apart: 5 -> 1, of which waited for: 4 -> 1; matrix products, arithmetic and copies ran while one was open for 1% -> 0% of each run, Pallas kernels for 12% -> 10%
where the time goes in v2:
time: 112 us
  blocking collectives  81 us (72%)
  Pallas kernels  18.8 us (17%)
  waiting for transfers between devices  4.42 us (4%)
  starting transfers between devices  3.51 us (3%)
  local copies, waits for them, and re-layouts  3.35 us (3%)
    all_to_all x2, blocking collectives, exchange(): return lax.all_to_all(value, axes, split_axis=0, concat_axis=0, tiled=True)  81 us
    pallas_call x4, Pallas kernels, vmem_call(): pl.pallas_call(kernel, out_shape=outs, in_specs=[pl.BlockSpec(memory_spac...  18.8 us
    all_to_all x1, waiting for transfers between devices, exchange(): return lax.all_to_all(value, axes, split_axis=0, concat_axis=0, tiled=True)  4.42 us
    all_to_all x1, starting transfers between devices, exchange(): return lax.all_to_all(value, axes, split_axis=0, concat_axis=0, tiled=True)  3.51 us
    unnamed x6, local copies, waits for them, and re-layouts  3.35 us
  transfers between devices with their start and end apart: 1, of which 1 were waited for; matrix products, arithmetic and copies ran while one was open for 0% of the time, Pallas kernels for 10%

profile of v2, /device:TPU:0, one launch (start us, length us, event | category | flops | bytes accessed | tf_op | source)
XLA Modules:
  0.0 111.8 jit_solution(18164392916970564447)
XLA Ops:
  0.6 0.0 copy-start
  0.6 1.2 %copy-done = f32[2048,128]{1,0:T(8,128)S(1)} copy-done((f32[2048,128]{1,0:T(8,128)S(1)}, f32[2048,128]{1,0:T(8,128)}, u32[]{:S(2)}) %copy-start) | copy-done | bytes 1048600
  1.9 0.0 copy-start.1
  1.9 1.2 %copy-done.1 = f32[2048,128]{1,0:T(8,128)S(1)} copy-done((f32[2048,128]{1,0:T(8,128)S(1)}, f32[2048,128]{1,0:T(8,128)}, u32[]{:S(2)}) %copy-start.1) | copy-done | bytes 1048600
  3.1 0.0 copy-start.2
  3.1 0.9 copy-done.2
  4.0 2.2 %pack_rows.1 = (f32[32,104,128]{2,1,0:T(8,128)S(1)}, f32[32,32,128]{2,1,0:T(8,128)}) custom-call(f32[2048,128]{1,0:T(8,128)S(1)} %copy-done, f32[2048,128]{1,0:T(8,128)S(1)} %copy-done.1, f32[256,128]{1,0:T(8,128)S(1)} %copy-done.2), custom_call_target="tpu_custom_call" | custom-call | flops 1000000 | bytes 2228224 | tf_op jit(solution)/shard_map/pack_rows/pallas_call | solution.py:136
  6.2 47.5 %all_to_all.15.refs_0_.refs_1_ = f32[32,104,128]{2,1,0:T(8,128)S(1)} all-to-all(f32[32,104,128]{2,1,0:T(8,128)S(1)} %get-tuple-element.6), channel_id=1, replica_groups=mesh['ctx'=16,'tp'=2] {'ctx','tp'}, dimensions={0} | all-to-all | bytes 3407872 | tf_op jit(solution)/shard_map/all_to_all | solution.py:207
  53.7 3.5 %all-to-all-start.1 = ((f32[32,32,128]{2,1,0:T(8,128)}), f32[32,32,128]{2,1,0:T(8,128)S(1)}, u32[]{:S(2)}, u32[]{:S(2)}) async-start(f32[32,32,128]{2,1,0:T(8,128)} %get-tuple-element.9), calls=%async_computation.1 | async-start | bytes 1048576 | tf_op jit(solution)/shard_map/all_to_all | solution.py:207
  57.2 11.1 %gradients.2.refs_2_ = f32[32,72,128]{2,1,0:T(8,128)S(1)} custom-call(f32[32,104,128]{2,1,0:T(8,128)S(1)} %all_to_all.15.refs_0_.refs_1_, f32[32,104,128]{2,1,0:T(8,128)S(1)} %all_to_all.15.refs_0_.refs_1_), custom_call_target="tpu_custom_call" | custom-call | flops 17999998976 | bytes 3407872 | tf_op jit(solution)/shard_map/gradients/pallas_call | solution.py:136
  68.3 4.4 %all-to-all-done.1.refs_1_ = f32[32,32,128]{2,1,0:T(8,128)S(1)} async-done(((f32[32,32,128]{2,1,0:T(8,128)}), f32[32,32,128]{2,1,0:T(8,128)S(1)}, u32[]{:S(2)}, u32[]{:S(2)}) %all-to-all-start.1) | async-done | bytes 524320 | tf_op jit(solution)/shard_map/all_to_all | solution.py:207
  72.7 3.8 %gradients.3 = f32[32,72,128]{2,1,0:T(8,128)S(1)} custom-call(f32[32,104,128]{2,1,0:T(8,128)S(1)} %all_to_all.15.refs_0_.refs_1_, f32[32,32,128]{2,1,0:T(8,128)S(1)} %all-to-all-done.1.refs_1_, f32[32,72,128]{2,1,0:T(8,128)S(1)} %gradients.2.refs_2_), custom_call_target="tpu_custom_call" | custom-call | flops 6000000000 | bytes 3407872 | tf_op jit(solution)/shard_map/gradients/pallas_call | solution.py:136
  76.5 33.5 %all_to_all.16.in_ref = f32[32,72,128]{2,1,0:T(8,128)S(1)} all-to-all(f32[32,72,128]{2,1,0:T(8,128)S(1)} %gradients.3), channel_id=1, replica_groups=mesh['ctx'=16,'tp'=2] {'ctx','tp'}, dimensions={0} | all-to-all | bytes 2359296 | tf_op jit(solution)/shard_map/all_to_all | solution.py:207
  110.1 1.7 %unpack_rows.1 = (f32[2048,128]{1,0:T(8,128)}, f32[256,128]{1,0:T(8,128)}) custom-call(f32[32,72,128]{2,1,0:T(8,128)S(1)} %all_to_all.16.in_ref), custom_call_target="tpu_custom_call" | custom-call | flops 1000000 | bytes 1179648 | tf_op jit(solution)/shard_map/unpack_rows/pallas_call | solution.py:136
Async XLA Ops:
  0.6 1.2 %copy-start = (f32[2048,128]{1,0:T(8,128)S(1)}, f32[2048,128]{1,0:T(8,128)}, u32[]{:S(2)}) copy-start(f32[2048,128]{1,0:T(8,128)} %cot_ref.1) | copy-start | bytes 3145732
  1.9 1.2 %copy-start.1 = (f32[2048,128]{1,0:T(8,128)S(1)}, f32[2048,128]{1,0:T(8,128)}, u32[]{:S(2)}) copy-start(f32[2048,128]{1,0:T(8,128)} %sig_ref.1) | copy-start | bytes 3145732
  3.1 0.9 copy-start.2
  53.7 19.1 %all-to-all-start.1 = ((f32[32,32,128]{2,1,0:T(8,128)}), f32[32,32,128]{2,1,0:T(8,128)S(1)}, u32[]{:S(2)}, u32[]{:S(2)}) async-start(f32[32,32,128]{2,1,0:T(8,128)} %get-tuple-element.9), calls=%async_computation.1 | async-start | bytes 1048576 | tf_op jit(solution)/shard_map/all_to_all | solution.py:207

commit v3 on v2

--- a/solution.py
+++ b/solution.py
@@ -1,4 +1,5 @@
 import functools
+import math
 
 import jax
 import jax.numpy as jnp
@@ -192,6 +193,109 @@
     lax.fori_loop(0, owners, one_owner, 0)
 
 
+def turn_blocks(value):
+    rows = [value[at] for at in range(8)]
+    sub = lax.broadcasted_iota(jnp.int32, rows[0].shape, 0)
+    for bit in (1, 2, 4):
+        clear = (sub & bit) == 0
+        turned = list(rows)
+        for at in range(8):
+            if at & bit == 0:
+                turned[at] = jnp.where(clear, rows[at], pltpu.roll(rows[at + bit], bit, 0))
+                turned[at + bit] = jnp.where(clear, pltpu.roll(rows[at], 8 - bit, 0), rows[at + bit])
+        rows = turned
+    return rows
+
+
+def pack_copied_kernel(plan, owners, chunks, cot_hbm, sig_hbm, fil_hbm, early_ref, late_ref, cot_ref, sig_ref, sems, fil_sem):
+    _, _, group, filts, early = plan
+    many = owners // chunks
+    span = many * filts
+    copies = []
+    for chunk in range(chunks):
+        for part, (source, target) in enumerate(((cot_hbm, cot_ref), (sig_hbm, sig_ref))):
+            rows = pl.ds(chunk * span, span)
+            copies.append(pltpu.make_async_copy(source.at[:, rows, :], target.at[:, rows, :], sems.at[part, chunk]))
+            copies[-1].start()
+    fil_copy = pltpu.make_async_copy(fil_hbm, early_ref.at[:, pl.ds(2 * early * group, filts), :], fil_sem)
+    fil_copy.start()
+    for chunk in range(chunks):
+        for part, source in enumerate((cot_ref, sig_ref)):
+            copies[2 * chunk + part].wait()
+            for owner in range(chunk * many, (chunk + 1) * many):
+                rows = turn_blocks(source[:, pl.ds(owner * filts, filts), :])
+                for filt in range(filts):
+                    if filt < early:
+                        early_ref[owner, pl.ds((part * early + filt) * group, group), :] = rows[filt]
+                    else:
+                        at = part * (filts - early) + filt - early
+                        late_ref[owner, pl.ds(at * group, group), :] = rows[filt]
+    fil_copy.wait()
+
+
+def unpack_copied_kernel(plan, owners, chunks, in_ref, sig_hbm, fil_hbm, sig_ref, sems, fil_sem):
+    _, _, group, filts, _ = plan
+    many = owners // chunks
+    span = many * filts
+    fil_copy = pltpu.make_async_copy(in_ref.at[:, pl.ds(filts * group, filts), :], fil_hbm, fil_sem)
+    fil_copy.start()
+    copies = []
+    for chunk in range(chunks):
+        for owner in range(chunk * many, (chunk + 1) * many):
+            block = jnp.stack([in_ref[owner, pl.ds(filt * group, group), :] for filt in range(filts)], axis=0)
+            for at, row in enumerate(turn_blocks(block)):
+                sig_ref[at, pl.ds(owner * filts, filts), :] = row
+        rows = pl.ds(chunk * span, span)
+        copies.append(pltpu.make_async_copy(sig_ref.at[:, rows, :], sig_hbm.at[:, rows, :], sems.at[chunk]))
+        copies[-1].start()
+    for copy in copies:
+        copy.wait()
+    fil_copy.wait()
+
+
+def pack_rows(plan, owners, sizes, cot, sig, fil):
+    _, _, group, filts, _ = plan
+    channels, local = cot.shape
+    outs = [jax.ShapeDtypeStruct((owners, rows, local), f32) for rows in sizes]
+    if (group, filts) != (8, 8):
+        return vmem_call(functools.partial(pack_kernel, plan, owners), outs, (cot, sig, fil), "pack_rows", 1e6)
+    chunks = math.gcd(owners, 4)
+    grouped = (group, channels // group, local)
+    return pl.pallas_call(
+        functools.partial(pack_copied_kernel, plan, owners, chunks),
+        out_shape=outs,
+        in_specs=[pl.BlockSpec(memory_space=pl.ANY)] * 3,
+        out_specs=[pl.BlockSpec(memory_space=pltpu.VMEM)] * 2,
+        scratch_shapes=[pltpu.VMEM(grouped, f32)] * 2
+        + [pltpu.SemaphoreType.DMA((2, chunks)), pltpu.SemaphoreType.DMA],
+        compiler_params=pltpu.CompilerParams(vmem_limit_bytes=61 << 20),
+        cost_estimate=pl.CostEstimate(flops=0, bytes_accessed=16 * cot.size, transcendentals=0),
+        name="pack_rows",
+    )(cot.reshape(grouped), sig.reshape(grouped), fil.reshape(owners, filts, local))
+
+
+def unpack_rows(plan, owners, value):
+    _, _, group, filts, _ = plan
+    count, local = owners * filts, value.shape[2]
+    channels = group * count
+    if (group, filts) != (8, 8):
+        outs = [jax.ShapeDtypeStruct((channels, local), f32), jax.ShapeDtypeStruct((count, local), f32)]
+        return vmem_call(functools.partial(unpack_kernel, plan, owners), outs, (value,), "unpack_rows", 1e6)
+    chunks = math.gcd(owners, 4)
+    grouped = (group, count, local)
+    dsig, dfil = pl.pallas_call(
+        functools.partial(unpack_copied_kernel, plan, owners, chunks),
+        out_shape=[jax.ShapeDtypeStruct(grouped, f32), jax.ShapeDtypeStruct((owners, filts, local), f32)],
+        in_specs=[pl.BlockSpec(memory_space=pltpu.VMEM)],
+        out_specs=[pl.BlockSpec(memory_space=pl.ANY)] * 2,
+        scratch_shapes=[pltpu.VMEM(grouped, f32), pltpu.SemaphoreType.DMA((chunks,)), pltpu.SemaphoreType.DMA],
+        compiler_params=pltpu.CompilerParams(vmem_limit_bytes=44 << 20),
+        cost_estimate=pl.CostEstimate(flops=0, bytes_accessed=8 * value.size, transcendentals=0),
+        name="unpack_rows",
+    )(value)
+    return dsig.reshape(channels, local), dfil.reshape(count, local)
+
+
 def body(signal, cotangent, filters):
     ranks, halves = lax.axis_size("ctx"), lax.axis_size("tp")
     channels, local = signal.shape
@@ -207,25 +311,13 @@
         return lax.all_to_all(value, axes, split_axis=0, concat_axis=0, tiled=True)
 
     sizes = (2 * early * group + filts, 2 * (filts - early) * group)
-    sends = vmem_call(
-        functools.partial(pack_kernel, plan, owners),
-        [jax.ShapeDtypeStruct((owners, rows, local), f32) for rows in sizes],
-        (cotangent, signal, filters),
-        "pack_rows",
-        1e6,
-    )
+    sends = pack_rows(plan, owners, sizes, cotangent, signal, filters)
     first = exchange(sends[0])
     first, late = lax.optimization_barrier((first, sends[1]))
     second = exchange(late)
     grads = call_gradients(plan, 0, early, first, first)
     grads = call_gradients(plan, early, filts, first, second, grads)
-    grad_signal, grad_filters = vmem_call(
-        functools.partial(unpack_kernel, plan, owners),
-        [jax.ShapeDtypeStruct((channels, local), f32), jax.ShapeDtypeStruct((count, local), f32)],
-        (exchange(grads),),
-        "unpack_rows",
-        1e6,
-    )
+    grad_signal, grad_filters = unpack_rows(plan, owners, exchange(grads))
     if not both:
         grad_filters = lax.psum(grad_filters, "tp")
     return grad_signal, grad_filters

time: 112 us -> 109 us (0.973)
  local copies, waits for them, and re-layouts: 3.35 us -> 0 us
    pallas_call x0 -> x2, Pallas kernels: none -> 4.09 us  [the longest x1 2.99 us: pack_rows(): pl.pallas_call(functools.partial(pack_copied_kernel, plan, owners, chunks...]
    pallas_call x4 -> x2, Pallas kernels: 18.8 us -> 14.9 us  [vmem_call(): pl.pallas_call(kernel, out_shape=outs, in_specs=[pl.BlockSpec(memory_spac...]
    unnamed x6 -> x0, local copies, waits for them, and re-layouts: 3.35 us -> none
where the time goes in v3:
time: 109 us
  blocking collectives  81.2 us (74%)
  Pallas kernels  19 us (17%)
  waiting for transfers between devices  4.42 us (4%)
  starting transfers between devices  3.51 us (3%)
    all_to_all x2, blocking collectives, exchange(): return lax.all_to_all(value, axes, split_axis=0, concat_axis=0, tiled=True)  81.2 us
    pallas_call x2, Pallas kernels, vmem_call(): pl.pallas_call(kernel, out_shape=outs, in_specs=[pl.BlockSpec(memory_spac...  14.9 us
    all_to_all x1, waiting for transfers between devices, exchange(): return lax.all_to_all(value, axes, split_axis=0, concat_axis=0, tiled=True)  4.42 us
    all_to_all x1, starting transfers between devices, exchange(): return lax.all_to_all(value, axes, split_axis=0, concat_axis=0, tiled=True)  3.51 us
    pallas_call x1, Pallas kernels, pack_rows(): pl.pallas_call(functools.partial(pack_copied_kernel, plan, owners, chunks...  2.99 us
  transfers between devices with their start and end apart: 1, of which 1 were waited for; matrix products, arithmetic and copies ran while one was open for 0% of the time, Pallas kernels for 10%

profile of v3, /device:TPU:0, one launch (start us, length us, event | category | flops | bytes accessed | tf_op | source)
XLA Modules:
  0.0 108.8 jit_solution(9468283581651891715)
XLA Ops:
  0.6 3.0 %pack_rows.1 = (f32[32,104,128]{2,1,0:T(8,128)}, f32[32,32,128]{2,1,0:T(8,128)}) custom-call(f32[8,256,128]{2,1,0:T(8,128)} %bitcast.5, f32[8,256,128]{2,1,0:T(8,128)} %bitcast.6, f32[32,8,128]{2,1,0:T(8,128)} %bitcast.7), custom_call_target="tpu_custom_call" | custom-call | bytes 4194304 | tf_op jit(solution)/shard_map/pack_rows/pallas_call | solution.py:264
  3.6 47.7 %all_to_all.15.refs_0_.refs_1_ = f32[32,104,128]{2,1,0:T(8,128)S(1)} all-to-all(f32[32,104,128]{2,1,0:T(8,128)} %get-tuple-element.8), channel_id=1, replica_groups=mesh['ctx'=16,'tp'=2] {'ctx','tp'}, dimensions={0} | all-to-all | bytes 3407872 | tf_op jit(solution)/shard_map/all_to_all | solution.py:311
  51.3 3.5 %all-to-all-start.1 = ((f32[32,32,128]{2,1,0:T(8,128)}), f32[32,32,128]{2,1,0:T(8,128)S(1)}, u32[]{:S(2)}, u32[]{:S(2)}) async-start(f32[32,32,128]{2,1,0:T(8,128)} %get-tuple-element.11), calls=%async_computation.1 | async-start | bytes 1048576 | tf_op jit(solution)/shard_map/all_to_all | solution.py:311
  54.9 11.1 %gradients.2.refs_2_ = f32[32,72,128]{2,1,0:T(8,128)S(1)} custom-call(f32[32,104,128]{2,1,0:T(8,128)S(1)} %all_to_all.15.refs_0_.refs_1_, f32[32,104,128]{2,1,0:T(8,128)S(1)} %all_to_all.15.refs_0_.refs_1_), custom_call_target="tpu_custom_call" | custom-call | flops 17999998976 | bytes 3407872 | tf_op jit(solution)/shard_map/gradients/pallas_call | solution.py:137
  66.0 4.4 %all-to-all-done.1.refs_1_ = f32[32,32,128]{2,1,0:T(8,128)S(1)} async-done(((f32[32,32,128]{2,1,0:T(8,128)}), f32[32,32,128]{2,1,0:T(8,128)S(1)}, u32[]{:S(2)}, u32[]{:S(2)}) %all-to-all-start.1) | async-done | bytes 524320 | tf_op jit(solution)/shard_map/all_to_all | solution.py:311
  70.4 3.8 %gradients.3 = f32[32,72,128]{2,1,0:T(8,128)S(1)} custom-call(f32[32,104,128]{2,1,0:T(8,128)S(1)} %all_to_all.15.refs_0_.refs_1_, f32[32,32,128]{2,1,0:T(8,128)S(1)} %all-to-all-done.1.refs_1_, f32[32,72,128]{2,1,0:T(8,128)S(1)} %gradients.2.refs_2_), custom_call_target="tpu_custom_call" | custom-call | flops 6000000000 | bytes 3407872 | tf_op jit(solution)/shard_map/gradients/pallas_call | solution.py:137
  74.2 33.5 %all_to_all.16.in_ref = f32[32,72,128]{2,1,0:T(8,128)S(1)} all-to-all(f32[32,72,128]{2,1,0:T(8,128)S(1)} %gradients.3), channel_id=1, replica_groups=mesh['ctx'=16,'tp'=2] {'ctx','tp'}, dimensions={0} | all-to-all | bytes 2359296 | tf_op jit(solution)/shard_map/all_to_all | solution.py:311
  107.7 1.1 %unpack_rows.1 = (f32[8,256,128]{2,1,0:T(8,128)}, f32[32,8,128]{2,1,0:T(8,128)}) custom-call(f32[32,72,128]{2,1,0:T(8,128)S(1)} %all_to_all.16.in_ref), custom_call_target="tpu_custom_call" | custom-call | bytes 2359296 | tf_op jit(solution)/shard_map/unpack_rows/pallas_call | solution.py:286
Async XLA Ops:
  51.3 19.1 %all-to-all-start.1 = ((f32[32,32,128]{2,1,0:T(8,128)}), f32[32,32,128]{2,1,0:T(8,128)S(1)}, u32[]{:S(2)}, u32[]{:S(2)}) async-start(f32[32,32,128]{2,1,0:T(8,128)} %get-tuple-element.11), calls=%async_computation.1 | async-start | bytes 1048576 | tf_op jit(solution)/shard_map/all_to_all | solution.py:311

commit v4 on v3

--- a/solution.py
+++ b/solution.py
@@ -38,10 +38,10 @@
 def gradients_kernel(plan, first_filt, last_filt, *refs):
     blocks, sources, group, filts, early = plan
     if first_filt == 0:
-        fil_ref, data_ref, out_ref, strip_high, strip_low, cot_high, cot_low, prod_ref = refs
+        fil_ref, data_ref, out_ref, strip_high, strip_low, cot_high, cot_low, weight_ref, prod_ref = refs
         fil_at = 2 * early * group
     else:
-        fil_ref, data_ref, done_ref, out_ref, strip_high, strip_low, cot_high, cot_low, prod_ref = refs
+        fil_ref, data_ref, done_ref, out_ref, strip_high, strip_low, cot_high, cot_low, weight_ref, prod_ref = refs
         fil_at = 2 * early * group
         out_ref[...] = done_ref[...]
     local = data_ref.shape[2]
@@ -53,12 +53,11 @@
     held = cot_high.dtype
     flip = lax.broadcasted_iota(jnp.int32, (local, local), 0) + lax.broadcasted_iota(jnp.int32, (local, local), 1)
     flip = jnp.where(flip == local - 1, 1.0, 0.0).astype(bf16)
-    for ref in (cot_high, cot_low):
-        ref[pl.ds(rows_all, rows_all), :] = jnp.zeros((rows_all, PAIR), held)
+    weight_ref[pl.ds(3 * rows_all, 256), :] = jnp.zeros((256, PAIR), held)
     prod_ref[pairs] = jnp.zeros((PAIR, PAIR), f32)
     lane = lax.broadcasted_iota(jnp.int32, (8, PAIR), 1)
-    sub = lax.broadcasted_iota(jnp.int32, (8, PAIR), 0)
-    ahead = lane - sub
+    sub = lax.broadcasted_iota(jnp.int32, (8 * pairs, PAIR), 0)
+    ahead = lane[:, :128] - sub[:8, :128]
 
     def one_filter(turn, carry):
         filt = first_filt + turn
@@ -66,6 +65,9 @@
         high, low = split_two(rows)
         cot_high[pl.ds(0, rows_all), :] = high.astype(held)
         cot_low[pl.ds(0, rows_all), :] = low.astype(held)
+        for at in range(0, rows_all, step_rows):
+            for turn_at, part in enumerate((high, low, high)):
+                weight_ref[pl.ds(3 * at + turn_at * step_rows, step_rows), :] = part[at : at + step_rows].astype(held)
 
         lags = [fil_ref[b * sources, pl.ds(fil_at + filt, 1), :] for b in reversed(range(blocks))]
         high, low = split_two(jnp.concatenate(lags, axis=0))
@@ -73,20 +75,24 @@
         back = [jnp.broadcast_to(back[b : b + 1, :], (8, local)) for b in range(blocks)]
         back = jnp.concatenate(back + [jnp.zeros((8, PAIR), f32)], axis=1)
         skewed = pltpu.roll(back, 1, 1, stride=1, stride_axis=0)
+        two = jnp.concatenate([skewed, pltpu.roll(skewed, 8, 1)], axis=0)
+        high, low = split_two(two)
+        high, low = high.astype(f32), low.astype(f32)
         for step in range(local // 16):
-            two = jnp.concatenate([pltpu.roll(skewed, 16 * step, 1), pltpu.roll(skewed, 16 * step + 8, 1)], axis=0)
-            high, low = split_two(two)
-            strip_high[pl.ds(16 * step, 16), :] = high
-            strip_low[pl.ds(16 * step, 16), :] = low
-
-        sig = load_blocks(data_ref, (count + turn) * group, blocks, sources, group).T
-        sig_high, sig_low = split_two(sig)
-        turned = jnp.concatenate([sig_high, sig_high, sig_low], axis=1)
+            strip_high[pl.ds(16 * step, 16), :] = pltpu.roll(high, 16 * step, 1).astype(bf16)
+            strip_low[pl.ds(16 * step, 16), :] = pltpu.roll(low, 16 * step, 1).astype(bf16)
+
+        sig = load_blocks(data_ref, (count + turn) * group, blocks, sources, group)
+        sig_high = sig.astype(bf16).astype(f32)
+        sig_low = sig - sig_high
+        stacked = []
+        for at in range(0, rows_all, step_rows):
+            stacked += [part[at : at + step_rows] for part in (sig_high, sig_high, sig_low)]
+        turned = jnp.concatenate(stacked, axis=0).T.astype(bf16)
         for gap in range(pairs):
-            high = cot_high[pl.ds(gap * step_rows, rows_all), :].astype(bf16)
-            low = cot_low[pl.ds(gap * step_rows, rows_all), :].astype(bf16)
-            weights = jnp.concatenate([high, low, high], axis=0)
-            prod_ref[gap] = jnp.dot(turned, weights, preferred_element_type=f32)
+            deep = min(-(-3 * (rows_all - gap * step_rows) // 256) * 256, 3 * rows_all)
+            weights = weight_ref[pl.ds(3 * gap * step_rows, deep), :].astype(bf16)
+            prod_ref[gap] = jnp.dot(turned[:, :deep], weights, preferred_element_type=f32)
 
         total = None
         for gap in range(pairs):
@@ -96,11 +102,8 @@
             at = length - gap * PAIR
             t_high = jnp.concatenate([strip_high[:, pl.ds(at, PAIR)], strip_high[:, pl.ds(at - local, PAIR)]], axis=0)
             t_low = jnp.concatenate([strip_low[:, pl.ds(at, PAIR)], strip_low[:, pl.ds(at - local, PAIR)]], axis=0)
-            part = (
-                jnp.dot(high, t_high, preferred_element_type=f32)
-                + jnp.dot(low, t_high, preferred_element_type=f32)
-                + jnp.dot(high, t_low, preferred_element_type=f32)
-            )
+            both = jnp.dot(jnp.concatenate([high, low], axis=0), t_high, preferred_element_type=f32)
+            part = both[:kept] + both[kept:] + jnp.dot(high, t_low, preferred_element_type=f32)
             if total is None:
                 total = part
             else:
@@ -112,22 +115,29 @@
                 piece = total[at : at + group, b % 2 * local : (b % 2 + 1) * local]
                 out_ref[b * sources + s, pl.ds(filt * group, group), :] = piece
 
-        def folded(gap, step, steps):
-            if steps == 1:
-                here = prod_ref[gap, pl.ds(8 * step, 8), :]
-                after = prod_ref[gap + 1, pl.ds(8 * step, 8), :]
-                return jnp.where(ahead >= 8 * step, here, after)
-            half = steps // 2
-            return folded(gap, step, half) + rotate_left(folded(gap, step + half, half), 8 * half)
-
+        def leaf(gap, step):
+            near, far = pl.ds(8 * step, 8), pl.ds(8 * step + 128, 8)
+            left, right = pl.ds(0, 128), pl.ds(128, 128)
+            valid = ahead >= 8 * step
+            first = jnp.where(valid, prod_ref[gap, near, left], prod_ref[gap + 1, near, left])
+            second = jnp.where(valid, prod_ref[gap, far, right], prod_ref[gap + 1, far, right])
+            return jnp.concatenate([first + second, prod_ref[gap, near, right] + prod_ref[gap + 1, far, left]], axis=1)
+
+        lagged = []
         for gap in range(pairs):
-            lagged = folded(gap, 0, PAIR // 8)
-            for bit in (1, 2, 4):
-                lagged = jnp.where((sub & bit) != 0, rotate_left(lagged, bit), lagged)
-            lagged = jnp.sum(lagged, axis=0, keepdims=True)
+            summed = leaf(gap, 0)
+            for step in range(1, PAIR // 16):
+                summed = summed + rotate_left(leaf(gap, step), 8 * step)
+            lagged.append(summed)
+        lagged = jnp.concatenate(lagged, axis=0)
+        for bit in (1, 2, 4):
+            lagged = jnp.where((sub & bit) != 0, rotate_left(lagged, bit), lagged)
+        lagged = jnp.sum(lagged.reshape(pairs, 8, PAIR), axis=1)
+        for gap in range(pairs):
             for s in range(sources):
-                out_ref[2 * gap * sources + s, pl.ds(filts * group + filt, 1), :] = lagged[:, :local]
-                out_ref[(2 * gap + 1) * sources + s, pl.ds(filts * group + filt, 1), :] = lagged[:, local:]
+                row = pl.ds(filts * group + filt, 1)
+                out_ref[2 * gap * sources + s, row, :] = lagged[gap : gap + 1, :local]
+                out_ref[(2 * gap + 1) * sources + s, row, :] = lagged[gap : gap + 1, local:]
         return carry
 
     lax.fori_loop(0, count, one_filter, 0)
@@ -155,8 +165,8 @@
     held = bf16 if sources * group % 16 == 0 else f32
     scratch = (
         [pltpu.VMEM((local, blocks * local + PAIR), bf16)] * 2
-        + [pltpu.VMEM((rows, PAIR), held)] * 2
-        + [pltpu.VMEM((blocks // 2 + 1, PAIR, PAIR), f32)]
+        + [pltpu.VMEM((rows // 2, PAIR), held)] * 2
+        + [pltpu.VMEM((3 * rows // 2 + 256, PAIR), held), pltpu.VMEM((blocks // 2 + 1, PAIR, PAIR), f32)]
     )
     outs = jax.ShapeDtypeStruct((blocks * sources, filts * group + filts, local), f32)
     kernel = functools.partial(gradients_kernel, plan, first_filt, last_filt)
@@ -304,7 +314,7 @@
     axes, sources = (("ctx", "tp"), halves) if both else ("ctx", 1)
     owners = ranks * sources
     group, filts = channels // count, count // owners
-    early = filts - filts // 4
+    early = filts - 1
     plan = (ranks, sources, group, filts, early)
 
     def exchange(value):

time: 109 us -> 109 us (level)
  blocking collectives: 81.2 us -> 88.7 us
  waiting for transfers between devices: 4.42 us -> 0.8 us
  Pallas kernels: 19 us -> 15.4 us
    all_to_all x2, blocking collectives: 81.2 us -> 88.7 us  [exchange(): return lax.all_to_all(value, axes, split_axis=0, concat_axis=0, tiled=True)]
    pallas_call x2, Pallas kernels: 14.9 us -> 11.3 us  [vmem_call(): pl.pallas_call(kernel, out_shape=outs, in_specs=[pl.BlockSpec(memory_spac...]
    all_to_all x1, waiting for transfers between devices: 4.42 us -> 0.8 us  [exchange(): return lax.all_to_all(value, axes, split_axis=0, concat_axis=0, tiled=True)]
  transfers between devices with their start and end apart: 1 -> 1, of which waited for: 1 -> 1; matrix products, arithmetic and copies ran while one was open for 0% -> 0% of each run, Pallas kernels for 10% -> 9%
where the time goes in v4:
time: 109 us
  blocking collectives  88.7 us (81%)
  Pallas kernels  15.4 us (14%)
  starting transfers between devices  3.62 us (3%)
    all_to_all x2, blocking collectives, exchange(): return lax.all_to_all(value, axes, split_axis=0, concat_axis=0, tiled=True)  88.7 us
    pallas_call x2, Pallas kernels, vmem_call(): pl.pallas_call(kernel, out_shape=outs, in_specs=[pl.BlockSpec(memory_spac...  11.3 us
    all_to_all x1, starting transfers between devices, exchange(): return lax.all_to_all(value, axes, split_axis=0, concat_axis=0, tiled=True)  3.62 us
    pallas_call x1, Pallas kernels, pack_rows(): pl.pallas_call(functools.partial(pack_copied_kernel, plan, owners, chunks...  2.99 us
  transfers between devices with their start and end apart: 1, of which 1 were waited for; matrix products, arithmetic and copies ran while one was open for 0% of the time, Pallas kernels for 9%

profile of v4, /device:TPU:0, one launch (start us, length us, event | category | flops | bytes accessed | tf_op | source)
XLA Modules:
  0.0 109.2 jit_solution(11171515286964836723)
XLA Ops:
  0.6 3.0 %pack_rows.1 = (f32[32,120,128]{2,1,0:T(8,128)}, f32[32,16,128]{2,1,0:T(8,128)}) custom-call(f32[8,256,128]{2,1,0:T(8,128)} %bitcast.5, f32[8,256,128]{2,1,0:T(8,128)} %bitcast.6, f32[32,8,128]{2,1,0:T(8,128)} %bitcast.7), custom_call_target="tpu_custom_call" | custom-call | bytes 4194304 | tf_op jit(solution)/shard_map/pack_rows/pallas_call | solution.py:274
  3.6 53.2 %all_to_all.15.refs_0_.refs_1_ = f32[32,120,128]{2,1,0:T(8,128)S(1)} all-to-all(f32[32,120,128]{2,1,0:T(8,128)} %get-tuple-element.8), channel_id=1, replica_groups=mesh['ctx'=16,'tp'=2] {'ctx','tp'}, dimensions={0} | all-to-all | bytes 3932160 | tf_op jit(solution)/shard_map/all_to_all | solution.py:321
  56.8 3.6 %all-to-all-start.1 = ((f32[32,16,128]{2,1,0:T(8,128)}), f32[32,16,128]{2,1,0:T(8,128)S(1)}, u32[]{:S(2)}, u32[]{:S(2)}) async-start(f32[32,16,128]{2,1,0:T(8,128)} %get-tuple-element.11), calls=%async_computation.1 | async-start | bytes 524288 | tf_op jit(solution)/shard_map/all_to_all | solution.py:321
  60.5 9.8 %gradients.2.refs_2_ = f32[32,72,128]{2,1,0:T(8,128)S(1)} custom-call(f32[32,120,128]{2,1,0:T(8,128)S(1)} %all_to_all.15.refs_0_.refs_1_, f32[32,120,128]{2,1,0:T(8,128)S(1)} %all_to_all.15.refs_0_.refs_1_), custom_call_target="tpu_custom_call" | custom-call | flops 20999999488 | bytes 3932160 | tf_op jit(solution)/shard_map/gradients/pallas_call | solution.py:147
  70.3 0.8 all-to-all-done.1.refs_1_
  71.1 1.5 %gradients.3 = f32[32,72,128]{2,1,0:T(8,128)S(1)} custom-call(f32[32,120,128]{2,1,0:T(8,128)S(1)} %all_to_all.15.refs_0_.refs_1_, f32[32,16,128]{2,1,0:T(8,128)S(1)} %all-to-all-done.1.refs_1_, f32[32,72,128]{2,1,0:T(8,128)S(1)} %gradients.2.refs_2_), custom_call_target="tpu_custom_call" | custom-call | flops 3000000000 | bytes 3407872 | tf_op jit(solution)/shard_map/gradients/pallas_call | solution.py:147
  72.5 35.5 %all_to_all.16.in_ref = f32[32,72,128]{2,1,0:T(8,128)S(1)} all-to-all(f32[32,72,128]{2,1,0:T(8,128)S(1)} %gradients.3), channel_id=1, replica_groups=mesh['ctx'=16,'tp'=2] {'ctx','tp'}, dimensions={0} | all-to-all | bytes 2359296 | tf_op jit(solution)/shard_map/all_to_all | solution.py:321
  108.1 1.1 %unpack_rows.1 = (f32[8,256,128]{2,1,0:T(8,128)}, f32[32,8,128]{2,1,0:T(8,128)}) custom-call(f32[32,72,128]{2,1,0:T(8,128)S(1)} %all_to_all.16.in_ref), custom_call_target="tpu_custom_call" | custom-call | bytes 2359296 | tf_op jit(solution)/shard_map/unpack_rows/pallas_call | solution.py:296
Async XLA Ops:
  56.8 14.2 %all-to-all-start.1 = ((f32[32,16,128]{2,1,0:T(8,128)}), f32[32,16,128]{2,1,0:T(8,128)S(1)}, u32[]{:S(2)}, u32[]{:S(2)}) async-start(f32[32,16,128]{2,1,0:T(8,128)} %get-tuple-element.11), calls=%async_computation.1 | async-start | bytes 524288 | tf_op jit(solution)/shard_map/all_to_all | solution.py:321

commit v5 on v4

--- a/solution.py
+++ b/solution.py
@@ -35,17 +35,9 @@
     return jnp.concatenate([even, odd], axis=1)
 
 
-def gradients_kernel(plan, first_filt, last_filt, *refs):
-    blocks, sources, group, filts, early = plan
-    if first_filt == 0:
-        fil_ref, data_ref, out_ref, strip_high, strip_low, cot_high, cot_low, weight_ref, prod_ref = refs
-        fil_at = 2 * early * group
-    else:
-        fil_ref, data_ref, done_ref, out_ref, strip_high, strip_low, cot_high, cot_low, weight_ref, prod_ref = refs
-        fil_at = 2 * early * group
-        out_ref[...] = done_ref[...]
+def gradients_kernel(plan, data_ref, out_ref, strip_high, strip_low, cot_high, cot_low, weight_ref, prod_ref):
+    blocks, sources, group, filts = plan
     local = data_ref.shape[2]
-    count = last_filt - first_filt
     pairs = blocks // 2
     step_rows = sources * group
     rows_all = pairs * step_rows
@@ -59,9 +51,8 @@
     sub = lax.broadcasted_iota(jnp.int32, (8 * pairs, PAIR), 0)
     ahead = lane[:, :128] - sub[:8, :128]
 
-    def one_filter(turn, carry):
-        filt = first_filt + turn
-        rows = load_blocks(data_ref, turn * group, blocks, sources, group)
+    def one_filter(filt, carry):
+        rows = load_blocks(data_ref, filt * group, blocks, sources, group)
         high, low = split_two(rows)
         cot_high[pl.ds(0, rows_all), :] = high.astype(held)
         cot_low[pl.ds(0, rows_all), :] = low.astype(held)
@@ -69,7 +60,7 @@
             for turn_at, part in enumerate((high, low, high)):
                 weight_ref[pl.ds(3 * at + turn_at * step_rows, step_rows), :] = part[at : at + step_rows].astype(held)
 
-        lags = [fil_ref[b * sources, pl.ds(fil_at + filt, 1), :] for b in reversed(range(blocks))]
+        lags = [data_ref[b * sources, pl.ds(2 * filts * group + filt, 1), :] for b in reversed(range(blocks))]
         high, low = split_two(jnp.concatenate(lags, axis=0))
         back = jnp.dot(high, flip, preferred_element_type=f32) + jnp.dot(low, flip, preferred_element_type=f32)
         back = [jnp.broadcast_to(back[b : b + 1, :], (8, local)) for b in range(blocks)]
@@ -82,7 +73,7 @@
             strip_high[pl.ds(16 * step, 16), :] = pltpu.roll(high, 16 * step, 1).astype(bf16)
             strip_low[pl.ds(16 * step, 16), :] = pltpu.roll(low, 16 * step, 1).astype(bf16)
 
-        sig = load_blocks(data_ref, (count + turn) * group, blocks, sources, group)
+        sig = load_blocks(data_ref, (filts + filt) * group, blocks, sources, group)
         sig_high = sig.astype(bf16).astype(f32)
         sig_low = sig - sig_high
         stacked = []
@@ -140,7 +131,7 @@
                 out_ref[(2 * gap + 1) * sources + s, row, :] = lagged[gap : gap + 1, local:]
         return carry
 
-    lax.fori_loop(0, count, one_filter, 0)
+    lax.fori_loop(0, filts, one_filter, 0)
 
 
 def vmem_call(kernel, outs, args, name, flops, scratch=()):
@@ -158,9 +149,9 @@
     )(*args)
 
 
-def call_gradients(plan, first_filt, last_filt, *args):
-    blocks, sources, group, filts, early = plan
-    local = args[0].shape[2]
+def call_gradients(plan, data):
+    blocks, sources, group, filts = plan
+    local = data.shape[2]
     rows = blocks * sources * group
     held = bf16 if sources * group % 16 == 0 else f32
     scratch = (
@@ -169,29 +160,27 @@
         + [pltpu.VMEM((3 * rows // 2 + 256, PAIR), held), pltpu.VMEM((blocks // 2 + 1, PAIR, PAIR), f32)]
     )
     outs = jax.ShapeDtypeStruct((blocks * sources, filts * group + filts, local), f32)
-    kernel = functools.partial(gradients_kernel, plan, first_filt, last_filt)
-    flops = (last_filt - first_filt) * 3e9
-    return vmem_call(kernel, outs, args, "gradients", flops, scratch)
-
-
-def pack_kernel(plan, owners, cot_ref, sig_ref, fil_ref, early_ref, late_ref):
-    _, _, group, filts, early = plan
+    kernel = functools.partial(gradients_kernel, plan)
+    return vmem_call(kernel, outs, (data,), "gradients", filts * 3e9, scratch)
+
+
+def pack_kernel(plan, owners, cot_ref, sig_ref, fil_ref, out_ref):
+    _, _, group, filts = plan
     count = owners * filts
 
     def one_owner(owner, carry):
         for filt in range(filts):
-            ref, at, many = (early_ref, filt, early) if filt < early else (late_ref, filt - early, filts - early)
             for part, source in enumerate((cot_ref, sig_ref)):
                 rows = source[pl.ds(owner * filts + filt, group, stride=count), :]
-                ref[owner, pl.ds((part * many + at) * group, group), :] = rows
-        early_ref[owner, pl.ds(2 * early * group, filts), :] = fil_ref[pl.ds(owner * filts, filts), :]
+                out_ref[owner, pl.ds((part * filts + filt) * group, group), :] = rows
+        out_ref[owner, pl.ds(2 * filts * group, filts), :] = fil_ref[pl.ds(owner * filts, filts), :]
         return carry
 
     lax.fori_loop(0, owners, one_owner, 0)
 
 
 def unpack_kernel(plan, owners, in_ref, sig_ref, fil_ref):
-    _, _, group, filts, _ = plan
+    _, _, group, filts = plan
     count = owners * filts
 
     def one_owner(owner, carry):
@@ -217,8 +206,8 @@
     return rows
 
 
-def pack_copied_kernel(plan, owners, chunks, cot_hbm, sig_hbm, fil_hbm, early_ref, late_ref, cot_ref, sig_ref, sems, fil_sem):
-    _, _, group, filts, early = plan
+def pack_copied_kernel(plan, owners, chunks, cot_hbm, sig_hbm, fil_hbm, out_ref, cot_ref, sig_ref, sems, fil_sem):
+    _, _, group, filts = plan
     many = owners // chunks
     span = many * filts
     copies = []
@@ -227,7 +216,7 @@
             rows = pl.ds(chunk * span, span)
             copies.append(pltpu.make_async_copy(source.at[:, rows, :], target.at[:, rows, :], sems.at[part, chunk]))
             copies[-1].start()
-    fil_copy = pltpu.make_async_copy(fil_hbm, early_ref.at[:, pl.ds(2 * early * group, filts), :], fil_sem)
+    fil_copy = pltpu.make_async_copy(fil_hbm, out_ref.at[:, pl.ds(2 * filts * group, filts), :], fil_sem)
     fil_copy.start()
     for chunk in range(chunks):
         for part, source in enumerate((cot_ref, sig_ref)):
@@ -235,16 +224,12 @@
             for owner in range(chunk * many, (chunk + 1) * many):
                 rows = turn_blocks(source[:, pl.ds(owner * filts, filts), :])
                 for filt in range(filts):
-                    if filt < early:
-                        early_ref[owner, pl.ds((part * early + filt) * group, group), :] = rows[filt]
-                    else:
-                        at = part * (filts - early) + filt - early
-                        late_ref[owner, pl.ds(at * group, group), :] = rows[filt]
+                    out_ref[owner, pl.ds((part * filts + filt) * group, group), :] = rows[filt]
     fil_copy.wait()
 
 
 def unpack_copied_kernel(plan, owners, chunks, in_ref, sig_hbm, fil_hbm, sig_ref, sems, fil_sem):
-    _, _, group, filts, _ = plan
+    _, _, group, filts = plan
     many = owners // chunks
     span = many * filts
     fil_copy = pltpu.make_async_copy(in_ref.at[:, pl.ds(filts * group, filts), :], fil_hbm, fil_sem)
@@ -263,19 +248,19 @@
     fil_copy.wait()
 
 
-def pack_rows(plan, owners, sizes, cot, sig, fil):
-    _, _, group, filts, _ = plan
+def pack_rows(plan, owners, cot, sig, fil):
+    _, _, group, filts = plan
     channels, local = cot.shape
-    outs = [jax.ShapeDtypeStruct((owners, rows, local), f32) for rows in sizes]
+    out = jax.ShapeDtypeStruct((owners, 2 * filts * group + filts, local), f32)
     if (group, filts) != (8, 8):
-        return vmem_call(functools.partial(pack_kernel, plan, owners), outs, (cot, sig, fil), "pack_rows", 1e6)
+        return vmem_call(functools.partial(pack_kernel, plan, owners), out, (cot, sig, fil), "pack_rows", 1e6)
     chunks = math.gcd(owners, 4)
     grouped = (group, channels // group, local)
     return pl.pallas_call(
         functools.partial(pack_copied_kernel, plan, owners, chunks),
-        out_shape=outs,
+        out_shape=out,
         in_specs=[pl.BlockSpec(memory_space=pl.ANY)] * 3,
-        out_specs=[pl.BlockSpec(memory_space=pltpu.VMEM)] * 2,
+        out_specs=pl.BlockSpec(memory_space=pltpu.VMEM),
         scratch_shapes=[pltpu.VMEM(grouped, f32)] * 2
         + [pltpu.SemaphoreType.DMA((2, chunks)), pltpu.SemaphoreType.DMA],
         compiler_params=pltpu.CompilerParams(vmem_limit_bytes=61 << 20),
@@ -285,7 +270,7 @@
 
 
 def unpack_rows(plan, owners, value):
-    _, _, group, filts, _ = plan
+    _, _, group, filts = plan
     count, local = owners * filts, value.shape[2]
     channels = group * count
     if (group, filts) != (8, 8):
@@ -314,20 +299,13 @@
     axes, sources = (("ctx", "tp"), halves) if both else ("ctx", 1)
     owners = ranks * sources
     group, filts = channels // count, count // owners
-    early = filts - 1
-    plan = (ranks, sources, group, filts, early)
+    plan = (ranks, sources, group, filts)
 
     def exchange(value):
         return lax.all_to_all(value, axes, split_axis=0, concat_axis=0, tiled=True)
 
-    sizes = (2 * early * group + filts, 2 * (filts - early) * group)
-    sends = pack_rows(plan, owners, sizes, cotangent, signal, filters)
-    first = exchange(sends[0])
-    first, late = lax.optimization_barrier((first, sends[1]))
-    second = exchange(late)
-    grads = call_gradients(plan, 0, early, first, first)
-    grads = call_gradients(plan, early, filts, first, second, grads)
-    grad_signal, grad_filters = unpack_rows(plan, owners, exchange(grads))
+    data = exchange(pack_rows(plan, owners, cotangent, signal, filters))
+    grad_signal, grad_filters = unpack_rows(plan, owners, exchange(call_gradients(plan, data)))
     if not both:
         grad_filters = lax.psum(grad_filters, "tp")
     return grad_signal, grad_filters

time: 109 us -> 109 us (level)
  blocking collectives: 88.7 us -> 93 us
  starting transfers between devices: 3.62 us -> 0 us
    all_to_all x2, blocking collectives: 88.7 us -> 93 us  [exchange(): return lax.all_to_all(value, axes, split_axis=0, concat_axis=0, tiled=True)]
    all_to_all x1 -> x0, starting transfers between devices: 3.62 us -> none  [exchange(): return lax.all_to_all(value, axes, split_axis=0, concat_axis=0, tiled=True)]
    pallas_call x2 -> x1, Pallas kernels: 11.3 us -> 11.2 us  [vmem_call(): pl.pallas_call(kernel, out_shape=outs, in_specs=[pl.BlockSpec(memory_spac...]
  transfers between devices with their start and end apart: 1 -> 0, of which waited for: 1 -> 0; matrix products, arithmetic and copies ran while one was open for 0% -> 0% of each run, Pallas kernels for 9% -> 0%
where the time goes in v5:
time: 109 us
  blocking collectives  93 us (85%)
  Pallas kernels  15.3 us (14%)
    all_to_all x2, blocking collectives, exchange(): return lax.all_to_all(value, axes, split_axis=0, concat_axis=0, tiled=True)  93 us
    pallas_call x1, Pallas kernels, vmem_call(): pl.pallas_call(kernel, out_shape=outs, in_specs=[pl.BlockSpec(memory_spac...  11.2 us
    pallas_call x1, Pallas kernels, pack_rows(): pl.pallas_call(functools.partial(pack_copied_kernel, plan, owners, chunks...  3.03 us

profile of v5, /device:TPU:0, one launch (start us, length us, event | category | flops | bytes accessed | tf_op | source)
XLA Modules:
  0.0 108.9 jit_solution(2858983578222490817)
XLA Ops:
  0.6 3.0 %pack_rows.1 = f32[32,136,128]{2,1,0:T(8,128)} custom-call(f32[8,256,128]{2,1,0:T(8,128)} %bitcast.5, f32[8,256,128]{2,1,0:T(8,128)} %bitcast.6, f32[32,8,128]{2,1,0:T(8,128)} %bitcast.7), custom_call_target="tpu_custom_call" | custom-call | bytes 4194304 | tf_op jit(solution)/shard_map/pack_rows/pallas_call | solution.py:259
  3.7 60.4 %all_to_all.10.data_ref = f32[32,136,128]{2,1,0:T(8,128)S(1)} all-to-all(f32[32,136,128]{2,1,0:T(8,128)} %pack_rows.1), channel_id=1, replica_groups=mesh['ctx'=16,'tp'=2] {'ctx','tp'}, dimensions={0} | all-to-all | bytes 4456448 | tf_op jit(solution)/shard_map/all_to_all | solution.py:305
  64.1 11.2 %gradients.1 = f32[32,72,128]{2,1,0:T(8,128)S(1)} custom-call(f32[32,136,128]{2,1,0:T(8,128)S(1)} %all_to_all.10.data_ref), custom_call_target="tpu_custom_call" | custom-call | flops 24000000000 | bytes 2228224 | tf_op jit(solution)/shard_map/gradients/pallas_call | solution.py:138
  75.3 32.5 %all_to_all.11.in_ref = f32[32,72,128]{2,1,0:T(8,128)S(1)} all-to-all(f32[32,72,128]{2,1,0:T(8,128)S(1)} %gradients.1), channel_id=1, replica_groups=mesh['ctx'=16,'tp'=2] {'ctx','tp'}, dimensions={0} | all-to-all | bytes 2359296 | tf_op jit(solution)/shard_map/all_to_all | solution.py:305
  107.8 1.1 %unpack_rows.1 = (f32[8,256,128]{2,1,0:T(8,128)}, f32[32,8,128]{2,1,0:T(8,128)}) custom-call(f32[32,72,128]{2,1,0:T(8,128)S(1)} %all_to_all.11.in_ref), custom_call_target="tpu_custom_call" | custom-call | bytes 2359296 | tf_op jit(solution)/shard_map/unpack_rows/pallas_call | solution.py:281

commit v6 on v5

--- a/solution.py
+++ b/solution.py
@@ -35,23 +35,30 @@
     return jnp.concatenate([even, odd], axis=1)
 
 
-def gradients_kernel(plan, data_ref, out_ref, strip_high, strip_low, cot_high, cot_low, weight_ref, prod_ref):
+def gradients_kernel(plan, data_ref, out_ref, lag_ref, *scratch):
+    slots = [scratch[at : at + 6] for at in range(0, len(scratch), 6)]
     blocks, sources, group, filts = plan
     local = data_ref.shape[2]
     pairs = blocks // 2
     step_rows = sources * group
     rows_all = pairs * step_rows
     length = blocks * local
-    held = cot_high.dtype
+    held = slots[0][2].dtype
     flip = lax.broadcasted_iota(jnp.int32, (local, local), 0) + lax.broadcasted_iota(jnp.int32, (local, local), 1)
     flip = jnp.where(flip == local - 1, 1.0, 0.0).astype(bf16)
-    weight_ref[pl.ds(3 * rows_all, 256), :] = jnp.zeros((256, PAIR), held)
-    prod_ref[pairs] = jnp.zeros((PAIR, PAIR), f32)
+    for *_, weight_ref, prod_ref in slots:
+        weight_ref[pl.ds(3 * rows_all, 256), :] = jnp.zeros((256, PAIR), held)
+        prod_ref[pairs] = jnp.zeros((PAIR, PAIR), f32)
     lane = lax.broadcasted_iota(jnp.int32, (8, PAIR), 1)
     sub = lax.broadcasted_iota(jnp.int32, (8 * pairs, PAIR), 0)
     ahead = lane[:, :128] - sub[:8, :128]
 
-    def one_filter(filt, carry):
+    for b in range(blocks):
+        high, low = split_two(data_ref[b * sources, pl.ds(2 * filts * group, filts), :])
+        lag_ref[b] = jnp.dot(high, flip, preferred_element_type=f32) + jnp.dot(low, flip, preferred_element_type=f32)
+
+    def one_filter(filt, slot):
+        strip_high, strip_low, cot_high, cot_low, weight_ref, prod_ref = slots[slot]
         rows = load_blocks(data_ref, filt * group, blocks, sources, group)
         high, low = split_two(rows)
         cot_high[pl.ds(0, rows_all), :] = high.astype(held)
@@ -60,10 +67,7 @@
             for turn_at, part in enumerate((high, low, high)):
                 weight_ref[pl.ds(3 * at + turn_at * step_rows, step_rows), :] = part[at : at + step_rows].astype(held)
 
-        lags = [data_ref[b * sources, pl.ds(2 * filts * group + filt, 1), :] for b in reversed(range(blocks))]
-        high, low = split_two(jnp.concatenate(lags, axis=0))
-        back = jnp.dot(high, flip, preferred_element_type=f32) + jnp.dot(low, flip, preferred_element_type=f32)
-        back = [jnp.broadcast_to(back[b : b + 1, :], (8, local)) for b in range(blocks)]
+        back = [jnp.broadcast_to(lag_ref[b, pl.ds(filt, 1), :], (8, local)) for b in reversed(range(blocks))]
         back = jnp.concatenate(back + [jnp.zeros((8, PAIR), f32)], axis=1)
         skewed = pltpu.roll(back, 1, 1, stride=1, stride_axis=0)
         two = jnp.concatenate([skewed, pltpu.roll(skewed, 8, 1)], axis=0)
@@ -129,9 +133,13 @@
                 row = pl.ds(filts * group + filt, 1)
                 out_ref[2 * gap * sources + s, row, :] = lagged[gap : gap + 1, :local]
                 out_ref[(2 * gap + 1) * sources + s, row, :] = lagged[gap : gap + 1, local:]
+
+    def some_filters(turn, carry):
+        for slot in range(len(slots)):
+            one_filter(turn * len(slots) + slot, slot)
         return carry
 
-    lax.fori_loop(0, filts, one_filter, 0)
+    lax.fori_loop(0, filts // len(slots), some_filters, 0)
 
 
 def vmem_call(kernel, outs, args, name, flops, scratch=()):
@@ -159,6 +167,7 @@
         + [pltpu.VMEM((rows // 2, PAIR), held)] * 2
         + [pltpu.VMEM((3 * rows // 2 + 256, PAIR), held), pltpu.VMEM((blocks // 2 + 1, PAIR, PAIR), f32)]
     )
+    scratch = [pltpu.VMEM((blocks, filts, local), f32)] + scratch * 2
     outs = jax.ShapeDtypeStruct((blocks * sources, filts * group + filts, local), f32)
     kernel = functools.partial(gradients_kernel, plan)
     return vmem_call(kernel, outs, (data,), "gradients", filts * 3e9, scratch)
@@ -263,10 +272,10 @@
         out_specs=pl.BlockSpec(memory_space=pltpu.VMEM),
         scratch_shapes=[pltpu.VMEM(grouped, f32)] * 2
         + [pltpu.SemaphoreType.DMA((2, chunks)), pltpu.SemaphoreType.DMA],
-        compiler_params=pltpu.CompilerParams(vmem_limit_bytes=61 << 20),
+        compiler_params=pltpu.CompilerParams(vmem_limit_bytes=44 << 20),
         cost_estimate=pl.CostEstimate(flops=0, bytes_accessed=16 * cot.size, transcendentals=0),
         name="pack_rows",
-    )(cot.reshape(grouped), sig.reshape(grouped), fil.reshape(owners, filts, local))
+    )(*[pltpu.with_memory_space_constraint(x, pltpu.HBM) for x in (cot.reshape(grouped), sig.reshape(grouped), fil.reshape(owners, filts, local))])
 
 
 def unpack_rows(plan, owners, value):

time: 109 us -> 105 us (0.963)
  Pallas kernels: 15.3 us -> 11.6 us
    pallas_call x1, Pallas kernels: 11.2 us -> 8.83 us  [vmem_call(): pl.pallas_call(kernel, out_shape=outs, in_specs=[pl.BlockSpec(memory_spac...]
    pallas_call x1, Pallas kernels: 3.03 us -> 1.64 us  [pack_rows(): pl.pallas_call(functools.partial(pack_copied_kernel, plan, owners, chunks...]
where the time goes in v6:
time: 105 us
  blocking collectives  92.8 us (88%)
  Pallas kernels  11.6 us (11%)
    all_to_all x2, blocking collectives, exchange(): return lax.all_to_all(value, axes, split_axis=0, concat_axis=0, tiled=True)  92.8 us
    pallas_call x1, Pallas kernels, vmem_call(): pl.pallas_call(kernel, out_shape=outs, in_specs=[pl.BlockSpec(memory_spac...  8.83 us

profile of v6, /device:TPU:0, one launch (start us, length us, event | category | flops | bytes accessed | tf_op | source)
XLA Modules:
  0.0 105.0 jit_solution(6309271326448569609)
XLA Ops:
  0.6 1.6 %pack_rows.1 = f32[32,136,128]{2,1,0:T(8,128)S(1)} custom-call(f32[8,256,128]{2,1,0:T(8,128)} %bitcast.5, f32[8,256,128]{2,1,0:T(8,128)} %bitcast.6, f32[32,8,128]{2,1,0:T(8,128)} %bitcast.7), custom_call_target="tpu_custom_call" | custom-call | bytes 4194304 | tf_op jit(solution)/shard_map/pack_rows/pallas_call | solution.py:268
  2.3 60.2 %all_to_all.10.data_ref = f32[32,136,128]{2,1,0:T(8,128)S(1)} all-to-all(f32[32,136,128]{2,1,0:T(8,128)S(1)} %pack_rows.1), channel_id=1, replica_groups=mesh['ctx'=16,'tp'=2] {'ctx','tp'}, dimensions={0} | all-to-all | bytes 4456448 | tf_op jit(solution)/shard_map/all_to_all | solution.py:314
  62.5 8.8 %gradients.1 = f32[32,72,128]{2,1,0:T(8,128)S(1)} custom-call(f32[32,136,128]{2,1,0:T(8,128)S(1)} %all_to_all.10.data_ref), custom_call_target="tpu_custom_call" | custom-call | flops 24000000000 | bytes 2228224 | tf_op jit(solution)/shard_map/gradients/pallas_call | solution.py:146
  71.3 32.5 %all_to_all.11.in_ref = f32[32,72,128]{2,1,0:T(8,128)S(1)} all-to-all(f32[32,72,128]{2,1,0:T(8,128)S(1)} %gradients.1), channel_id=1, replica_groups=mesh['ctx'=16,'tp'=2] {'ctx','tp'}, dimensions={0} | all-to-all | bytes 2359296 | tf_op jit(solution)/shard_map/all_to_all | solution.py:314
  103.9 1.1 %unpack_rows.1 = (f32[8,256,128]{2,1,0:T(8,128)}, f32[32,8,128]{2,1,0:T(8,128)}) custom-call(f32[32,72,128]{2,1,0:T(8,128)S(1)} %all_to_all.11.in_ref), custom_call_target="tpu_custom_call" | custom-call | bytes 2359296 | tf_op jit(solution)/shard_map/unpack_rows/pallas_call | solution.py:290

commit v7 on v6

--- a/solution.py
+++ b/solution.py
@@ -85,7 +85,7 @@
             stacked += [part[at : at + step_rows] for part in (sig_high, sig_high, sig_low)]
         turned = jnp.concatenate(stacked, axis=0).T.astype(bf16)
         for gap in range(pairs):
-            deep = min(-(-3 * (rows_all - gap * step_rows) // 256) * 256, 3 * rows_all)
+            deep = min(-(-3 * (rows_all - gap * step_rows) // 128) * 128, 3 * rows_all)
             weights = weight_ref[pl.ds(3 * gap * step_rows, deep), :].astype(bf16)
             prod_ref[gap] = jnp.dot(turned[:, :deep], weights, preferred_element_type=f32)
 
@@ -167,7 +167,7 @@
         + [pltpu.VMEM((rows // 2, PAIR), held)] * 2
         + [pltpu.VMEM((3 * rows // 2 + 256, PAIR), held), pltpu.VMEM((blocks // 2 + 1, PAIR, PAIR), f32)]
     )
-    scratch = [pltpu.VMEM((blocks, filts, local), f32)] + scratch * 2
+    scratch = [pltpu.VMEM((blocks, filts, local), f32)] + scratch * (2 if filts % 2 == 0 else 1)
     outs = jax.ShapeDtypeStruct((blocks * sources, filts * group + filts, local), f32)
     kernel = functools.partial(gradients_kernel, plan)
     return vmem_call(kernel, outs, (data,), "gradients", filts * 3e9, scratch)

time: 105 us -> 105 us (level)
  no operation moved by 1% of the time
where the time goes in v7:
time: 105 us
  blocking collectives  92.8 us (88%)
  Pallas kernels  11.3 us (11%)
    all_to_all x2, blocking collectives, exchange(): return lax.all_to_all(value, axes, split_axis=0, concat_axis=0, tiled=True)  92.8 us
    pallas_call x1, Pallas kernels, vmem_call(): pl.pallas_call(kernel, out_shape=outs, in_specs=[pl.BlockSpec(memory_spac...  8.59 us

profile of v7, /device:TPU:0, one launch (start us, length us, event | category | flops | bytes accessed | tf_op | source)
XLA Modules:
  0.0 104.7 jit_solution(15251136769282593306)
XLA Ops:
  0.6 1.6 %pack_rows.1 = f32[32,136,128]{2,1,0:T(8,128)S(1)} custom-call(f32[8,256,128]{2,1,0:T(8,128)} %bitcast.5, f32[8,256,128]{2,1,0:T(8,128)} %bitcast.6, f32[32,8,128]{2,1,0:T(8,128)} %bitcast.7), custom_call_target="tpu_custom_call" | custom-call | bytes 4194304 | tf_op jit(solution)/shard_map/pack_rows/pallas_call | solution.py:268
  2.3 60.2 %all_to_all.10.data_ref = f32[32,136,128]{2,1,0:T(8,128)S(1)} all-to-all(f32[32,136,128]{2,1,0:T(8,128)S(1)} %pack_rows.1), channel_id=1, replica_groups=mesh['ctx'=16,'tp'=2] {'ctx','tp'}, dimensions={0} | all-to-all | bytes 4456448 | tf_op jit(solution)/shard_map/all_to_all | solution.py:314
  62.5 8.6 %gradients.1 = f32[32,72,128]{2,1,0:T(8,128)S(1)} custom-call(f32[32,136,128]{2,1,0:T(8,128)S(1)} %all_to_all.10.data_ref), custom_call_target="tpu_custom_call" | custom-call | flops 24000000000 | bytes 2228224 | tf_op jit(solution)/shard_map/gradients/pallas_call | solution.py:146
  71.1 32.5 %all_to_all.11.in_ref = f32[32,72,128]{2,1,0:T(8,128)S(1)} all-to-all(f32[32,72,128]{2,1,0:T(8,128)S(1)} %gradients.1), channel_id=1, replica_groups=mesh['ctx'=16,'tp'=2] {'ctx','tp'}, dimensions={0} | all-to-all | bytes 2359296 | tf_op jit(solution)/shard_map/all_to_all | solution.py:314
  103.6 1.1 %unpack_rows.1 = (f32[8,256,128]{2,1,0:T(8,128)}, f32[32,8,128]{2,1,0:T(8,128)}) custom-call(f32[32,72,128]{2,1,0:T(8,128)S(1)} %all_to_all.11.in_ref), custom_call_target="tpu_custom_call" | custom-call | bytes 2359296 | tf_op jit(solution)/shard_map/unpack_rows/pallas_call | solution.py:290

commit v8 on v7

--- a/solution.py
+++ b/solution.py
@@ -25,11 +25,18 @@
     return pltpu.roll(value, value.shape[1] - shift, 1)
 
 
+def load_tile(ref, owner, start, group):
+    if len(ref.shape) == 3:
+        return ref[owner, pl.ds(start, group), :]
+    high = ref.shape[2]
+    return ref[owner, pl.ds(start // high, group // high), :, :].reshape(group, ref.shape[3])
+
+
 def load_blocks(ref, start, blocks, sources, group):
     pieces = []
     for b in range(blocks):
         for s in range(sources):
-            pieces.append(ref[b * sources + s, pl.ds(start, group), :])
+            pieces.append(load_tile(ref, b * sources + s, start, group))
     even = jnp.concatenate([p for at, p in enumerate(pieces) if at // sources % 2 == 0], axis=0)
     odd = jnp.concatenate([p for at, p in enumerate(pieces) if at // sources % 2 == 1], axis=0)
     return jnp.concatenate([even, odd], axis=1)
@@ -38,7 +45,7 @@
 def gradients_kernel(plan, data_ref, out_ref, lag_ref, *scratch):
     slots = [scratch[at : at + 6] for at in range(0, len(scratch), 6)]
     blocks, sources, group, filts = plan
-    local = data_ref.shape[2]
+    local = data_ref.shape[-1]
     pairs = blocks // 2
     step_rows = sources * group
     rows_all = pairs * step_rows
@@ -54,7 +61,12 @@
     ahead = lane[:, :128] - sub[:8, :128]
 
     for b in range(blocks):
-        high, low = split_two(data_ref[b * sources, pl.ds(2 * filts * group, filts), :])
+        if len(data_ref.shape) == 3:
+            lags = data_ref[b * sources, pl.ds(2 * filts * group, filts), :]
+        else:
+            parts = [data_ref[b * sources + s, 2 * filts * group // (filts // sources)] for s in range(sources)]
+            lags = jnp.concatenate(parts, axis=0)
+        high, low = split_two(lags)
         lag_ref[b] = jnp.dot(high, flip, preferred_element_type=f32) + jnp.dot(low, flip, preferred_element_type=f32)
 
     def one_filter(filt, slot):
@@ -159,7 +171,7 @@
 
 def call_gradients(plan, data):
     blocks, sources, group, filts = plan
-    local = data.shape[2]
+    local = data.shape[-1]
     rows = blocks * sources * group
     held = bf16 if sources * group % 16 == 0 else f32
     scratch = (
@@ -215,8 +227,9 @@
     return rows
 
 
-def pack_copied_kernel(plan, owners, chunks, cot_hbm, sig_hbm, fil_hbm, out_ref, cot_ref, sig_ref, sems, fil_sem):
-    _, _, group, filts = plan
+def pack_copied_kernel(plan, owners, chunks, cot_hbm, sig_hbm, fil_hbm, out_ref, cot_ref, sig_ref, fil_ref, sems, fil_sem):
+    _, sources, group, filts = plan
+    share = filts // sources
     many = owners // chunks
     span = many * filts
     copies = []
@@ -225,7 +238,7 @@
             rows = pl.ds(chunk * span, span)
             copies.append(pltpu.make_async_copy(source.at[:, rows, :], target.at[:, rows, :], sems.at[part, chunk]))
             copies[-1].start()
-    fil_copy = pltpu.make_async_copy(fil_hbm, out_ref.at[:, pl.ds(2 * filts * group, filts), :], fil_sem)
+    fil_copy = pltpu.make_async_copy(fil_hbm, fil_ref, fil_sem)
     fil_copy.start()
     for chunk in range(chunks):
         for part, source in enumerate((cot_ref, sig_ref)):
@@ -233,8 +246,15 @@
             for owner in range(chunk * many, (chunk + 1) * many):
                 rows = turn_blocks(source[:, pl.ds(owner * filts, filts), :])
                 for filt in range(filts):
-                    out_ref[owner, pl.ds((part * filts + filt) * group, group), :] = rows[filt]
+                    at = (part * filts + filt) * group // share
+                    out_ref[owner, pl.ds(at, group // share), :, :] = rows[filt].reshape(group // share, share, -1)
     fil_copy.wait()
+    mine = lax.axis_index("tp")
+    for owner in range(owners):
+        kept = fil_ref[owner, pl.ds(0, share), :]
+        for s in range(1, sources):
+            kept = jnp.where(mine == s, fil_ref[owner, pl.ds(s * share, share), :], kept)
+        out_ref[owner, 2 * filts * group // share] = kept
 
 
 def unpack_copied_kernel(plan, owners, chunks, in_ref, sig_hbm, fil_hbm, sig_ref, sems, fil_sem):
@@ -258,11 +278,13 @@
 
 
 def pack_rows(plan, owners, cot, sig, fil):
-    _, _, group, filts = plan
+    _, sources, group, filts = plan
     channels, local = cot.shape
     out = jax.ShapeDtypeStruct((owners, 2 * filts * group + filts, local), f32)
-    if (group, filts) != (8, 8):
+    if (sources, group, filts) != (2, 8, 8):
         return vmem_call(functools.partial(pack_kernel, plan, owners), out, (cot, sig, fil), "pack_rows", 1e6)
+    share = filts // sources
+    out = jax.ShapeDtypeStruct((owners, 2 * filts * group // share + 1, share, local), f32)
     chunks = math.gcd(owners, 4)
     grouped = (group, channels // group, local)
     return pl.pallas_call(
@@ -271,6 +293,7 @@
         in_specs=[pl.BlockSpec(memory_space=pl.ANY)] * 3,
         out_specs=pl.BlockSpec(memory_space=pltpu.VMEM),
         scratch_shapes=[pltpu.VMEM(grouped, f32)] * 2
+        + [pltpu.VMEM((owners, filts, local), f32)]
         + [pltpu.SemaphoreType.DMA((2, chunks)), pltpu.SemaphoreType.DMA],
         compiler_params=pltpu.CompilerParams(vmem_limit_bytes=44 << 20),
         cost_estimate=pl.CostEstimate(flops=0, bytes_accessed=16 * cot.size, transcendentals=0),

time: 105 us -> 104 us (level)
  blocking collectives: 92.8 us -> 91.3 us
    all_to_all x2, blocking collectives: 92.8 us -> 91.3 us  [exchange(): return lax.all_to_all(value, axes, split_axis=0, concat_axis=0, tiled=True)]
where the time goes in v8:
time: 104 us; the launch traced here: 103 us
  blocking collectives  91.3 us (88%)
  Pallas kernels  11.5 us (11%)
    all_to_all x2, blocking collectives, exchange(): return lax.all_to_all(value, axes, split_axis=0, concat_axis=0, tiled=True)  91.3 us
    pallas_call x1, Pallas kernels, vmem_call(): pl.pallas_call(kernel, out_shape=outs, in_specs=[pl.BlockSpec(memory_spac...  8.69 us

profile of v8, /device:TPU:0, one launch (start us, length us, event | category | flops | bytes accessed | tf_op | source)
XLA Modules:
  0.0 103.4 jit_solution(16722236656616435244)
XLA Ops:
  0.6 1.7 %pack_rows.1 = f32[32,33,4,128]{3,2,1,0:T(4,128)S(1)} custom-call(f32[8,256,128]{2,1,0:T(8,128)} %bitcast.5, f32[8,256,128]{2,1,0:T(8,128)} %bitcast.6, f32[32,8,128]{2,1,0:T(8,128)} %bitcast.7), custom_call_target="tpu_custom_call" | custom-call | bytes 4194304 | tf_op jit(solution)/shard_map/pack_rows/pallas_call | solution.py:290
  2.3 58.9 %all_to_all.10.data_ref = f32[32,33,4,128]{3,2,1,0:T(4,128)S(1)} all-to-all(f32[32,33,4,128]{3,2,1,0:T(4,128)S(1)} %pack_rows.1), channel_id=1, replica_groups=mesh['ctx'=16,'tp'=2] {'ctx','tp'}, dimensions={0} | all-to-all | bytes 4325376 | tf_op jit(solution)/shard_map/all_to_all | solution.py:337
  61.2 8.7 %gradients.1 = f32[32,72,128]{2,1,0:T(8,128)S(1)} custom-call(f32[32,33,4,128]{3,2,1,0:T(4,128)S(1)} %all_to_all.10.data_ref), custom_call_target="tpu_custom_call" | custom-call | flops 24000000000 | bytes 2162688 | tf_op jit(solution)/shard_map/gradients/pallas_call | solution.py:158
  69.9 32.4 %all_to_all.11.in_ref = f32[32,72,128]{2,1,0:T(8,128)S(1)} all-to-all(f32[32,72,128]{2,1,0:T(8,128)S(1)} %gradients.1), channel_id=1, replica_groups=mesh['ctx'=16,'tp'=2] {'ctx','tp'}, dimensions={0} | all-to-all | bytes 2359296 | tf_op jit(solution)/shard_map/all_to_all | solution.py:337
  102.3 1.1 %unpack_rows.1 = (f32[8,256,128]{2,1,0:T(8,128)}, f32[32,8,128]{2,1,0:T(8,128)}) custom-call(f32[32,72,128]{2,1,0:T(8,128)S(1)} %all_to_all.11.in_ref), custom_call_target="tpu_custom_call" | custom-call | bytes 2359296 | tf_op jit(solution)/shard_map/unpack_rows/pallas_call | solution.py:313

commit v9 on v8

--- a/solution.py
+++ b/solution.py
@@ -100,6 +100,7 @@
             deep = min(-(-3 * (rows_all - gap * step_rows) // 128) * 128, 3 * rows_all)
             weights = weight_ref[pl.ds(3 * gap * step_rows, deep), :].astype(bf16)
             prod_ref[gap] = jnp.dot(turned[:, :deep], weights, preferred_element_type=f32)
+            yield
 
         total = None
         for gap in range(pairs):
@@ -147,8 +148,9 @@
                 out_ref[(2 * gap + 1) * sources + s, row, :] = lagged[gap : gap + 1, local:]
 
     def some_filters(turn, carry):
-        for slot in range(len(slots)):
-            one_filter(turn * len(slots) + slot, slot)
+        stages = [one_filter(turn * len(slots) + slot, slot) for slot in range(len(slots))]
+        while stages:
+            stages = [stage for stage in stages if next(stage, 1) is None]
         return carry
 
     lax.fori_loop(0, filts // len(slots), some_filters, 0)

time: 104 us -> 103 us (level)
  no operation moved by 1% of the time
where the time goes in v9:
time: 103 us
  blocking collectives  91.3 us (89%)
  Pallas kernels  11.3 us (11%)
    all_to_all x2, blocking collectives, exchange(): return lax.all_to_all(value, axes, split_axis=0, concat_axis=0, tiled=True)  91.3 us
    pallas_call x1, Pallas kernels, vmem_call(): pl.pallas_call(kernel, out_shape=outs, in_specs=[pl.BlockSpec(memory_spac...  8.53 us

profile of v9, /device:TPU:0, one launch (start us, length us, event | category | flops | bytes accessed | tf_op | source)
XLA Modules:
  0.0 103.3 jit_solution(13440291617839177235)
XLA Ops:
  0.6 1.7 %pack_rows.1 = f32[32,33,4,128]{3,2,1,0:T(4,128)S(1)} custom-call(f32[8,256,128]{2,1,0:T(8,128)} %bitcast.5, f32[8,256,128]{2,1,0:T(8,128)} %bitcast.6, f32[32,8,128]{2,1,0:T(8,128)} %bitcast.7), custom_call_target="tpu_custom_call" | custom-call | bytes 4194304 | tf_op jit(solution)/shard_map/pack_rows/pallas_call | solution.py:292
  2.3 58.9 %all_to_all.10.data_ref = f32[32,33,4,128]{3,2,1,0:T(4,128)S(1)} all-to-all(f32[32,33,4,128]{3,2,1,0:T(4,128)S(1)} %pack_rows.1), channel_id=1, replica_groups=mesh['ctx'=16,'tp'=2] {'ctx','tp'}, dimensions={0} | all-to-all | bytes 4325376 | tf_op jit(solution)/shard_map/all_to_all | solution.py:339
  61.2 8.5 %gradients.1 = f32[32,72,128]{2,1,0:T(8,128)S(1)} custom-call(f32[32,33,4,128]{3,2,1,0:T(4,128)S(1)} %all_to_all.10.data_ref), custom_call_target="tpu_custom_call" | custom-call | flops 24000000000 | bytes 2162688 | tf_op jit(solution)/shard_map/gradients/pallas_call | solution.py:160
  69.8 32.4 %all_to_all.11.in_ref = f32[32,72,128]{2,1,0:T(8,128)S(1)} all-to-all(f32[32,72,128]{2,1,0:T(8,128)S(1)} %gradients.1), channel_id=1, replica_groups=mesh['ctx'=16,'tp'=2] {'ctx','tp'}, dimensions={0} | all-to-all | bytes 2359296 | tf_op jit(solution)/shard_map/all_to_all | solution.py:339
  102.2 1.1 %unpack_rows.1 = (f32[8,256,128]{2,1,0:T(8,128)}, f32[32,8,128]{2,1,0:T(8,128)}) custom-call(f32[32,72,128]{2,1,0:T(8,128)S(1)} %all_to_all.11.in_ref), custom_call_target="tpu_custom_call" | custom-call | bytes 2359296 | tf_op jit(solution)/shard_map/unpack_rows/pallas_call | solution.py:315

commit v10 on v9

--- a/solution.py
+++ b/solution.py
@@ -137,6 +137,7 @@
             for step in range(1, PAIR // 16):
                 summed = summed + rotate_left(leaf(gap, step), 8 * step)
             lagged.append(summed)
+            yield
         lagged = jnp.concatenate(lagged, axis=0)
         for bit in (1, 2, 4):
             lagged = jnp.where((sub & bit) != 0, rotate_left(lagged, bit), lagged)

time: 103 us -> 103 us (level)
  no operation moved by 1% of the time
where the time goes in v10:
time: 103 us
  blocking collectives  91.3 us (89%)
  Pallas kernels  11 us (11%)
    all_to_all x2, blocking collectives, exchange(): return lax.all_to_all(value, axes, split_axis=0, concat_axis=0, tiled=True)  91.3 us
    pallas_call x1, Pallas kernels, vmem_call(): pl.pallas_call(kernel, out_shape=outs, in_specs=[pl.BlockSpec(memory_spac...  8.24 us

profile of v10, /device:TPU:0, one launch (start us, length us, event | category | flops | bytes accessed | tf_op | source)
XLA Modules:
  0.0 103.0 jit_solution(17771165308994211848)
XLA Ops:
  0.6 1.7 %pack_rows.1 = f32[32,33,4,128]{3,2,1,0:T(4,128)S(1)} custom-call(f32[8,256,128]{2,1,0:T(8,128)} %bitcast.5, f32[8,256,128]{2,1,0:T(8,128)} %bitcast.6, f32[32,8,128]{2,1,0:T(8,128)} %bitcast.7), custom_call_target="tpu_custom_call" | custom-call | bytes 4194304 | tf_op jit(solution)/shard_map/pack_rows/pallas_call | solution.py:293
  2.3 58.9 %all_to_all.10.data_ref = f32[32,33,4,128]{3,2,1,0:T(4,128)S(1)} all-to-all(f32[32,33,4,128]{3,2,1,0:T(4,128)S(1)} %pack_rows.1), channel_id=1, replica_groups=mesh['ctx'=16,'tp'=2] {'ctx','tp'}, dimensions={0} | all-to-all | bytes 4325376 | tf_op jit(solution)/shard_map/all_to_all | solution.py:340
  61.2 8.2 %gradients.1 = f32[32,72,128]{2,1,0:T(8,128)S(1)} custom-call(f32[32,33,4,128]{3,2,1,0:T(4,128)S(1)} %all_to_all.10.data_ref), custom_call_target="tpu_custom_call" | custom-call | flops 24000000000 | bytes 2162688 | tf_op jit(solution)/shard_map/gradients/pallas_call | solution.py:161
  69.5 32.4 %all_to_all.11.in_ref = f32[32,72,128]{2,1,0:T(8,128)S(1)} all-to-all(f32[32,72,128]{2,1,0:T(8,128)S(1)} %gradients.1), channel_id=1, replica_groups=mesh['ctx'=16,'tp'=2] {'ctx','tp'}, dimensions={0} | all-to-all | bytes 2359296 | tf_op jit(solution)/shard_map/all_to_all | solution.py:340
  101.9 1.1 %unpack_rows.1 = (f32[8,256,128]{2,1,0:T(8,128)}, f32[32,8,128]{2,1,0:T(8,128)}) custom-call(f32[32,72,128]{2,1,0:T(8,128)S(1)} %all_to_all.11.in_ref), custom_call_target="tpu_custom_call" | custom-call | bytes 2359296 | tf_op jit(solution)/shard_map/unpack_rows/pallas_call | solution.py:316
